TPU v7x, 128 devices: a whole 4x4x4 slice. The times are simulated.
128 devices in a mesh: section: 8 (over z_hi, x), tp: 16 (over y, z_lo, core).
Axes of the slice: x: 4, y: 4, z: 4 (z_hi: 2, z_lo: 2; z = z_hi * 2 + z_lo), core: 2. Of those that a mesh axis runs over, the one named last changes fastest.
Arguments:
- hidden_in: bfloat16 [2, 128, 8192], P(None, None, 'tp'), may hold values from -11.25 to 11.25
- norm_gain: float32 [8, 8192], P('section'), may hold values from 0.5 to 2
- w_query: bfloat16 [8, 8192, 8192], P('section', None, 'tp'), may hold values from -0.375 to 2.125
- w_key_value: bfloat16 [8, 8192, 2048], P('section', None, 'tp'), may hold values from -0.0625 to 0.0625
- w_out: bfloat16 [8, 8192, 8192], P('section', 'tp'), may hold values from -0.0625 to 0.0625
- cache: bfloat16 [8, 2, 16384, 256], P('section', None, 'tp'), may hold values from -6 to 6
- ctx_len: int32 [2], replicated, may hold values from 512 to 2048, as said below
- placement: int32 [8, 8, 2], P('section'), may hold values from 0 to 15, as said below
Outputs:
- layer_outputs: bfloat16 [8, 2, 128, 8192], P('section', None, None, 'tp')
- kv_store: bfloat16 [8, 32, 128, 256], P('section', 'tp')
Inputs may be any that keep to these rules, and one draw needn't show every extreme that they name: `ctx_len`: one micro-batch has exactly 2048 cached tokens. `placement`: no holder receives more than 2 blocks of one layer, and in every layer some holder receives exactly 2.
All inputs are finite; a program needn't handle non-finite values.
Results may differ from a plain program's by a relative error of at most 0.028.
Values may be sent and summed in bfloat16 or wider, within the bound.
No kernel may reach another device: no remote copies, remote signals or barrier semaphores. Data moves between devices by JAX's collectives and lax.ppermute only.
A program may use at most 64 MiB of HBM per device.

v0:
```python
import math

import jax
import jax.numpy as jnp
from jax import lax
from jax.sharding import PartitionSpec as P

KVH = 8
HD = 128
SLOTS = 2


def partner(x, axis, stride):
    return lax.ppermute(x, axis, [(i, i ^ 1 << stride) for i in range(lax.axis_size(axis))])


def shifted(block, axis, distance):
    devices = range(lax.axis_size(axis))
    route = [(i - distance, i) for i in devices if i - distance in devices]
    return lax.ppermute(block, axis, route)


def rotate(values, positions):
    half = values.shape[-1] // 2
    freqs = jnp.exp(
        jnp.arange(half, dtype=jnp.float32) * (-2.0 * math.log(500000.0) / values.shape[-1])
    )
    angles = positions.astype(jnp.float32)[:, None] * freqs[None, :]
    shape = (angles.shape[0],) + (1,) * (values.ndim - 2) + (half,)
    cosine = jnp.cos(angles).reshape(shape)
    sine = jnp.sin(angles).reshape(shape)
    first = values[..., :half]
    second = values[..., half:]
    return jnp.concatenate(
        [first * cosine - second * sine, second * cosine + first * sine], axis=-1
    )


def collect_cache(piece, member_rank):
    stacked = piece[None]
    other = partner(stacked, "tp", 0)
    upper = member_rank >> 0 & 1 == 1
    stacked = jnp.where(
        upper, jnp.concatenate([other, stacked], 0), jnp.concatenate([stacked, other], 0)
    )
    return stacked


def collect_columns(piece, member_rank):
    stacked = piece[None]
    other = partner(stacked.astype(jnp.bfloat16), "tp", 0).astype(stacked.dtype)
    upper = member_rank >> 0 & 1 == 1
    stacked = jnp.where(
        upper, jnp.concatenate([other, stacked], 0), jnp.concatenate([stacked, other], 0)
    )
    return stacked


def shards(hidden_in, norm_gain, w_query, w_key_value, w_out, cache, ctx_len, placement):
    n_section = lax.axis_size("section")
    n_tp = lax.axis_size("tp")
    section = lax.axis_index("section")
    member = lax.axis_index("tp")
    group = n_tp // KVH
    member_rank = member % group
    micro, span, local_width = hidden_in.shape
    head_dim = HD
    query_weight = w_query[0]
    pair_weight = w_key_value[0]
    out_weight = w_out[0]
    gain = norm_gain[0]
    dev_heads = query_weight.shape[1] // head_dim
    quarter = cache.shape[2]
    rows = span // group
    root = math.sqrt(head_dim)
    causal = jnp.arange(span)[None, :] <= jnp.arange(span)[:, None]
    whole_cache = collect_cache(cache[0], member_rank)
    whole_cache = jnp.moveaxis(whole_cache, 0, 1).reshape(micro, group * quarter, 2 * head_dim)

    def tick(step, carry):
        incoming, outputs, pieces = carry
        micro_index = step - section
        valid = (micro_index >= 0) & (micro_index < micro)
        current = jnp.clip(micro_index, 0, micro - 1)
        first_in = lax.dynamic_index_in_dim(hidden_in, current, 0, keepdims=False)
        layer_in = jnp.where(section == 0, first_in, incoming)
        features = lax.all_gather(layer_in, "tp", axis=1, tiled=True)
        wide = features.astype(jnp.float32)
        normed = (
            wide * lax.rsqrt(jnp.mean(wide * wide, axis=-1, keepdims=True) + 1e-05) * gain
        ).astype(jnp.bfloat16)
        query_sum = jnp.dot(normed, query_weight, preferred_element_type=jnp.float32)
        pair_sum = jnp.dot(normed, pair_weight, preferred_element_type=jnp.float32)
        length = lax.dynamic_index_in_dim(ctx_len, current, 0, keepdims=False)
        positions = length + jnp.arange(span, dtype=jnp.int32)
        queries = rotate(query_sum.reshape(span, dev_heads, head_dim), positions).astype(
            jnp.bfloat16
        )
        columns = pair_sum.reshape(span, 2, head_dim // group)
        columns = collect_columns(columns, member_rank)
        columns = jnp.transpose(columns, (1, 2, 0, 3)).reshape(span, 2, head_dim)
        fresh_keys = rotate(columns[:, 0], positions).astype(jnp.bfloat16)
        fresh_values = columns[:, 1].astype(jnp.bfloat16)
        fresh_scores = (
            jnp.einsum("qhd,kd->hqk", queries, fresh_keys, preferred_element_type=jnp.float32)
            / root
        )
        fresh_scores = jnp.where(causal[None], fresh_scores, -1e30)
        context = lax.dynamic_index_in_dim(whole_cache, current, 0, keepdims=False)
        live = jnp.arange(context.shape[0]) < length
        cached_scores = (
            jnp.einsum(
                "qhd,kd->hqk", queries, context[:, :head_dim], preferred_element_type=jnp.float32
            )
            / root
        )
        cached_scores = jnp.where(live[None, None, :], cached_scores, -1e30)
        top = jnp.maximum(jnp.max(cached_scores, axis=-1), jnp.max(fresh_scores, axis=-1))
        cached_weights = jnp.exp(cached_scores - top[..., None])
        fresh_weights = jnp.exp(fresh_scores - top[..., None])
        total = jnp.sum(cached_weights, axis=-1) + jnp.sum(fresh_weights, axis=-1)
        mixed = jnp.einsum(
            "hqk,kd->hqd",
            cached_weights.astype(jnp.bfloat16),
            context[:, head_dim:],
            preferred_element_type=jnp.float32,
        )
        mixed = mixed + jnp.einsum(
            "hqk,kd->hqd",
            fresh_weights.astype(jnp.bfloat16),
            fresh_values,
            preferred_element_type=jnp.float32,
        )
        attended = (
            jnp.transpose(mixed / total[..., None], (1, 0, 2))
            .reshape(span, dev_heads * head_dim)
            .astype(jnp.bfloat16)
        )
        partial_value = jnp.dot(attended, out_weight, preferred_element_type=jnp.float32)
        summed = lax.psum_scatter(
            partial_value.astype(jnp.bfloat16), "tp", scatter_dimension=1, tiled=True
        ).astype(jnp.float32)
        updated = (layer_in.astype(jnp.float32) + summed).astype(jnp.bfloat16)
        outputs = jnp.where(
            valid, lax.dynamic_update_index_in_dim(outputs, updated, current, 0), outputs
        )
        joined = jnp.concatenate([fresh_keys, fresh_values], axis=-1)
        piece = lax.dynamic_slice_in_dim(joined, member_rank * rows, rows, 0)
        pieces = jnp.where(
            valid, lax.dynamic_update_index_in_dim(pieces, piece, current, 0), pieces
        )
        passed = shifted(updated, "section", 1)
        return (passed, outputs, pieces)

    start = (
        jnp.zeros((span, local_width), jnp.bfloat16),
        jnp.zeros((micro, span, local_width), jnp.bfloat16),
        jnp.zeros((micro, rows, 2 * head_dim), jnp.bfloat16),
    )
    passed_last, outputs, pieces = lax.fori_loop(0, n_section + micro - 1, tick, start)
    gathered = lax.all_gather(pieces[None], "tp", axis=0, tiled=True)
    blocks = gathered.reshape(KVH, group, micro, rows, 2 * head_dim)
    blocks = jnp.transpose(blocks, (0, 2, 1, 3, 4)).reshape(KVH * micro, span, 2 * head_dim)
    holders = placement[0].reshape(-1)
    count = holders.shape[0]
    earlier = (holders[None, :] == holders[:, None]) & (
        jnp.arange(count)[None, :] < jnp.arange(count)[:, None]
    )
    ranks = jnp.sum(earlier.astype(jnp.int32), axis=-1)
    chosen = ((holders[None, :] == member) & (ranks[None, :] == jnp.arange(SLOTS)[:, None])).astype(
        jnp.bfloat16
    )
    store = jnp.einsum("se,erc->src", chosen, blocks, preferred_element_type=jnp.float32).astype(
        jnp.bfloat16
    )
    return (outputs[None], store[None])


def solution(mesh):
    in_specs = (
        P(None, None, "tp"),
        P("section", None),
        P("section", None, "tp"),
        P("section", None, "tp"),
        P("section", "tp", None),
        P("section", None, "tp", None),
        P(),
        P("section", None, None),
    )
    out_specs = (P("section", None, None, "tp"), P("section", "tp", None, None))
    return jax.shard_map(shards, mesh=mesh, in_specs=in_specs, out_specs=out_specs, check_vma=False)
```

profile of v0, /device:TPU:73, one launch (start us, length us, event | category | flops | bytes accessed | tf_op | source)
XLA Modules:
  0.0 1221.9 jit_solution(15901497934529986805)
XLA Ops:
  14.7 1153.4 %while.20 = (s32[]{:T(128)}, bf16[128,512]{1,0:T(8,128)(2,1)S(1)}, bf16[2,128,512]{2,1,0:T(8,128)(2,1)}, bf16[2,64,256]{2,1,0:T(8,128)(2,1)}, pred[]{:T(512)}, /...) while((s32[]{:T(128)}, bf16[128,512]{1,0:T(8,128)(2,1)S(1)}, ...), condition=%wide.region_7.8_spmd.clone, body=%wide.region_0.7_spmd.clone.sunk | while | flops 3012699648 | bytes 116894416 | solution.py:160
  18.7 34.0 %all-gather.6.cloned.1.call-done = bf16[128,8192]{1,0:T(8,128)(2,1)} async-done(((bf16[128,512]{1,0:T(8,128)(2,1)}), bf16[128,8192]{1,0:T(8,128)(2,1)}) %all-gather.6.cloned.1.call-update) | async-done | bytes 2097168 | tf_op jit(solution)/shard_map/while/body/eval_jaxpr/all_gather | solution.py:87
  54.9 6.2 fusion.83
  73.2 53.5 %reduce-scatter.2.cloned.1.call-done = bf16[128,512]{1,0:T(8,128)(2,1)} async-done(((bf16[128,8192]{1,0:T(8,128)(2,1)}), bf16[128,512]{1,0:T(8,128)(2,1)}) %reduce-scatter.2.cloned.1.call-update) | async-done | bytes 131088 | tf_op jit(solution)/shard_map/while/body/eval_jaxpr/reduce_scatter | solution.py:140
  141.0 40.9 %all-gather.6.cloned.1.call-done = bf16[128,8192]{1,0:T(8,128)(2,1)} async-done(((bf16[128,512]{1,0:T(8,128)(2,1)}), bf16[128,8192]{1,0:T(8,128)(2,1)}) %all-gather.6.cloned.1.call-update) | async-done | bytes 2097168 | tf_op jit(solution)/shard_map/while/body/eval_jaxpr/all_gather | solution.py:87
  184.1 6.2 fusion.83
  202.4 53.5 %reduce-scatter.2.cloned.1.call-done = bf16[128,512]{1,0:T(8,128)(2,1)} async-done(((bf16[128,8192]{1,0:T(8,128)(2,1)}), bf16[128,512]{1,0:T(8,128)(2,1)}) %reduce-scatter.2.cloned.1.call-update) | async-done | bytes 131088 | tf_op jit(solution)/shard_map/while/body/eval_jaxpr/reduce_scatter | solution.py:140
  260.1 6.0 collective-permute-done.1
  270.3 40.3 %all-gather.6.cloned.1.call-done = bf16[128,8192]{1,0:T(8,128)(2,1)} async-done(((bf16[128,512]{1,0:T(8,128)(2,1)}), bf16[128,8192]{1,0:T(8,128)(2,1)}) %all-gather.6.cloned.1.call-update) | async-done | bytes 2097168 | tf_op jit(solution)/shard_map/while/body/eval_jaxpr/all_gather | solution.py:87
  312.7 6.2 fusion.83
  331.0 53.3 %reduce-scatter.2.cloned.1.call-done = bf16[128,512]{1,0:T(8,128)(2,1)} async-done(((bf16[128,8192]{1,0:T(8,128)(2,1)}), bf16[128,512]{1,0:T(8,128)(2,1)}) %reduce-scatter.2.cloned.1.call-update) | async-done | bytes 131088 | tf_op jit(solution)/shard_map/while/body/eval_jaxpr/reduce_scatter | solution.py:140
  398.8 40.8 %all-gather.6.cloned.1.call-done = bf16[128,8192]{1,0:T(8,128)(2,1)} async-done(((bf16[128,512]{1,0:T(8,128)(2,1)}), bf16[128,8192]{1,0:T(8,128)(2,1)}) %all-gather.6.cloned.1.call-update) | async-done | bytes 2097168 | tf_op jit(solution)/shard_map/while/body/eval_jaxpr/all_gather | solution.py:87
  441.7 6.2 fusion.83
  460.0 53.5 %reduce-scatter.2.cloned.1.call-done = bf16[128,512]{1,0:T(8,128)(2,1)} async-done(((bf16[128,8192]{1,0:T(8,128)(2,1)}), bf16[128,512]{1,0:T(8,128)(2,1)}) %reduce-scatter.2.cloned.1.call-update) | async-done | bytes 131088 | tf_op jit(solution)/shard_map/while/body/eval_jaxpr/reduce_scatter | solution.py:140
  527.9 40.8 %all-gather.6.cloned.1.call-done = bf16[128,8192]{1,0:T(8,128)(2,1)} async-done(((bf16[128,512]{1,0:T(8,128)(2,1)}), bf16[128,8192]{1,0:T(8,128)(2,1)}) %all-gather.6.cloned.1.call-update) | async-done | bytes 2097168 | tf_op jit(solution)/shard_map/while/body/eval_jaxpr/all_gather | solution.py:87
  570.8 6.2 fusion.83
  589.1 53.5 %reduce-scatter.2.cloned.1.call-done = bf16[128,512]{1,0:T(8,128)(2,1)} async-done(((bf16[128,8192]{1,0:T(8,128)(2,1)}), bf16[128,512]{1,0:T(8,128)(2,1)}) %reduce-scatter.2.cloned.1.call-update) | async-done | bytes 131088 | tf_op jit(solution)/shard_map/while/body/eval_jaxpr/reduce_scatter | solution.py:140
  657.0 40.7 %all-gather.6.cloned.1.call-done = bf16[128,8192]{1,0:T(8,128)(2,1)} async-done(((bf16[128,512]{1,0:T(8,128)(2,1)}), bf16[128,8192]{1,0:T(8,128)(2,1)}) %all-gather.6.cloned.1.call-update) | async-done | bytes 2097168 | tf_op jit(solution)/shard_map/while/body/eval_jaxpr/all_gather | solution.py:87
  699.8 6.2 fusion.83
  718.1 53.5 %reduce-scatter.2.cloned.1.call-done = bf16[128,512]{1,0:T(8,128)(2,1)} async-done(((bf16[128,8192]{1,0:T(8,128)(2,1)}), bf16[128,512]{1,0:T(8,128)(2,1)}) %reduce-scatter.2.cloned.1.call-update) | async-done | bytes 131088 | tf_op jit(solution)/shard_map/while/body/eval_jaxpr/reduce_scatter | solution.py:140
  786.0 40.6 %all-gather.6.cloned.1.call-done = bf16[128,8192]{1,0:T(8,128)(2,1)} async-done(((bf16[128,512]{1,0:T(8,128)(2,1)}), bf16[128,8192]{1,0:T(8,128)(2,1)}) %all-gather.6.cloned.1.call-update) | async-done | bytes 2097168 | tf_op jit(solution)/shard_map/while/body/eval_jaxpr/all_gather | solution.py:87
  828.7 6.2 fusion.83
  847.1 53.5 %reduce-scatter.2.cloned.1.call-done = bf16[128,512]{1,0:T(8,128)(2,1)} async-done(((bf16[128,8192]{1,0:T(8,128)(2,1)}), bf16[128,512]{1,0:T(8,128)(2,1)}) %reduce-scatter.2.cloned.1.call-update) | async-done | bytes 131088 | tf_op jit(solution)/shard_map/while/body/eval_jaxpr/reduce_scatter | solution.py:140
  914.9 40.4 %all-gather.6.cloned.1.call-done = bf16[128,8192]{1,0:T(8,128)(2,1)} async-done(((bf16[128,512]{1,0:T(8,128)(2,1)}), bf16[128,8192]{1,0:T(8,128)(2,1)}) %all-gather.6.cloned.1.call-update) | async-done | bytes 2097168 | tf_op jit(solution)/shard_map/while/body/eval_jaxpr/all_gather | solution.py:87
  957.4 6.2 fusion.83
  975.7 53.4 %reduce-scatter.2.cloned.1.call-done = bf16[128,512]{1,0:T(8,128)(2,1)} async-done(((bf16[128,8192]{1,0:T(8,128)(2,1)}), bf16[128,512]{1,0:T(8,128)(2,1)}) %reduce-scatter.2.cloned.1.call-update) | async-done | bytes 131088 | tf_op jit(solution)/shard_map/while/body/eval_jaxpr/reduce_scatter | solution.py:140
  1033.5 6.0 collective-permute-done.1
  1043.6 40.4 %all-gather.6.cloned.1.call-done = bf16[128,8192]{1,0:T(8,128)(2,1)} async-done(((bf16[128,512]{1,0:T(8,128)(2,1)}), bf16[128,8192]{1,0:T(8,128)(2,1)}) %all-gather.6.cloned.1.call-update) | async-done | bytes 2097168 | tf_op jit(solution)/shard_map/while/body/eval_jaxpr/all_gather | solution.py:87
  1086.1 6.2 fusion.83
  1104.4 53.4 %reduce-scatter.2.cloned.1.call-done = bf16[128,512]{1,0:T(8,128)(2,1)} async-done(((bf16[128,8192]{1,0:T(8,128)(2,1)}), bf16[128,512]{1,0:T(8,128)(2,1)}) %reduce-scatter.2.cloned.1.call-update) | async-done | bytes 131088 | tf_op jit(solution)/shard_map/while/body/eval_jaxpr/reduce_scatter | solution.py:140
  1162.1 6.0 collective-permute-done.1
  1169.1 41.6 %all-gather.4.cloned.1.call-done = bf16[32,64,256]{2,1,0:T(8,128)(2,1)} async-done(((bf16[2,64,256]{2,1,0:T(8,128)(2,1)}), bf16[32,64,256]{2,1,0:T(8,128)(2,1)}) %all-gather.4.cloned.1.call-update) | async-done | bytes 1048592 | tf_op jit(solution)/shard_map/all_gather | solution.py:161
  (603 shorter events, 247.6 us)
Async XLA Ops:
  8.0 3.3 collective-permute-start.2
  14.7 38.1 %all-gather.6.cloned.1.call-start = ((), (), s32[]{:S(2)}) async-start(), calls=%async_computation.2 | async-start | bytes 2228224 | tf_op jit(solution)/shard_map/while/body/eval_jaxpr/all_gather | solution.py:87
  16.5 110.1 %reduce-scatter.2.cloned.1.call-start = ((), (), s32[]{:S(2)}) async-start(), calls=%async_computation.3 | async-start | bytes 2228224 | tf_op jit(solution)/shard_map/while/body/eval_jaxpr/reduce_scatter | solution.py:140
  64.8 1.3 collective-permute-start
  127.6 9.3 collective-permute-start.1
  137.0 45.0 %all-gather.6.cloned.1.call-start = ((), (), s32[]{:S(2)}) async-start(), calls=%async_computation.2 | async-start | bytes 2228224 | tf_op jit(solution)/shard_map/while/body/eval_jaxpr/all_gather | solution.py:87
  138.8 117.1 %reduce-scatter.2.cloned.1.call-start = ((), (), s32[]{:S(2)}) async-start(), calls=%async_computation.3 | async-start | bytes 2228224 | tf_op jit(solution)/shard_map/while/body/eval_jaxpr/reduce_scatter | solution.py:140
  194.0 1.3 collective-permute-start
  256.9 9.3 collective-permute-start.1
  266.2 44.4 %all-gather.6.cloned.1.call-start = ((), (), s32[]{:S(2)}) async-start(), calls=%async_computation.2 | async-start | bytes 2228224 | tf_op jit(solution)/shard_map/while/body/eval_jaxpr/all_gather | solution.py:87
  268.0 116.3 %reduce-scatter.2.cloned.1.call-start = ((), (), s32[]{:S(2)}) async-start(), calls=%async_computation.3 | async-start | bytes 2228224 | tf_op jit(solution)/shard_map/while/body/eval_jaxpr/reduce_scatter | solution.py:140
  322.7 1.3 collective-permute-start
  385.4 9.3 collective-permute-start.1
  394.7 44.9 %all-gather.6.cloned.1.call-start = ((), (), s32[]{:S(2)}) async-start(), calls=%async_computation.2 | async-start | bytes 2228224 | tf_op jit(solution)/shard_map/while/body/eval_jaxpr/all_gather | solution.py:87
  396.5 117.0 %reduce-scatter.2.cloned.1.call-start = ((), (), s32[]{:S(2)}) async-start(), calls=%async_computation.3 | async-start | bytes 2228224 | tf_op jit(solution)/shard_map/while/body/eval_jaxpr/reduce_scatter | solution.py:140
  514.5 9.3 collective-permute-start.1
  523.8 44.8 %all-gather.6.cloned.1.call-start = ((), (), s32[]{:S(2)}) async-start(), calls=%async_computation.2 | async-start | bytes 2228224 | tf_op jit(solution)/shard_map/while/body/eval_jaxpr/all_gather | solution.py:87
  525.7 116.9 %reduce-scatter.2.cloned.1.call-start = ((), (), s32[]{:S(2)}) async-start(), calls=%async_computation.3 | async-start | bytes 2228224 | tf_op jit(solution)/shard_map/while/body/eval_jaxpr/reduce_scatter | solution.py:140
  643.6 9.3 collective-permute-start.1
  652.9 44.8 %all-gather.6.cloned.1.call-start = ((), (), s32[]{:S(2)}) async-start(), calls=%async_computation.2 | async-start | bytes 2228224 | tf_op jit(solution)/shard_map/while/body/eval_jaxpr/all_gather | solution.py:87
  654.7 116.9 %reduce-scatter.2.cloned.1.call-start = ((), (), s32[]{:S(2)}) async-start(), calls=%async_computation.3 | async-start | bytes 2228224 | tf_op jit(solution)/shard_map/while/body/eval_jaxpr/reduce_scatter | solution.py:140
  772.6 9.3 collective-permute-start.1
  781.9 44.7 %all-gather.6.cloned.1.call-start = ((), (), s32[]{:S(2)}) async-start(), calls=%async_computation.2 | async-start | bytes 2228224 | tf_op jit(solution)/shard_map/while/body/eval_jaxpr/all_gather | solution.py:87
  783.8 116.8 %reduce-scatter.2.cloned.1.call-start = ((), (), s32[]{:S(2)}) async-start(), calls=%async_computation.3 | async-start | bytes 2228224 | tf_op jit(solution)/shard_map/while/body/eval_jaxpr/reduce_scatter | solution.py:140
  901.5 9.3 collective-permute-start.1
  910.9 44.4 %all-gather.6.cloned.1.call-start = ((), (), s32[]{:S(2)}) async-start(), calls=%async_computation.2 | async-start | bytes 2228224 | tf_op jit(solution)/shard_map/while/body/eval_jaxpr/all_gather | solution.py:87
  912.7 116.5 %reduce-scatter.2.cloned.1.call-start = ((), (), s32[]{:S(2)}) async-start(), calls=%async_computation.3 | async-start | bytes 2228224 | tf_op jit(solution)/shard_map/while/body/eval_jaxpr/reduce_scatter | solution.py:140
  1030.1 9.3 collective-permute-start.1
  1039.5 44.4 %all-gather.6.cloned.1.call-start = ((), (), s32[]{:S(2)}) async-start(), calls=%async_computation.2 | async-start | bytes 2228224 | tf_op jit(solution)/shard_map/while/body/eval_jaxpr/all_gather | solution.py:87
  1041.3 116.5 %reduce-scatter.2.cloned.1.call-start = ((), (), s32[]{:S(2)}) async-start(), calls=%async_computation.3 | async-start | bytes 2228224 | tf_op jit(solution)/shard_map/while/body/eval_jaxpr/reduce_scatter | solution.py:140
  1158.8 9.3 collective-permute-start.1
  1168.1 42.6 %all-gather.4.cloned.1.call-start = ((), (), s32[]{:S(2)}) async-start(), calls=%async_computation.1 | async-start | bytes 1114112 | tf_op jit(solution)/shard_map/all_gather | solution.py:161
  (98 other events, 3477.9 us)
Sparse Core Ops, SparseCore 0:
  17.7 34.9 all-gather.5
  73.1 53.4 reduce-scatter.1
  140.0 41.8 all-gather.5
  202.3 53.5 reduce-scatter.1
  269.0 41.5 all-gather.5
  331.0 53.3 reduce-scatter.1
  397.8 41.7 all-gather.5
  460.0 53.4 reduce-scatter.1
  526.9 41.7 all-gather.5
  589.0 53.4 reduce-scatter.1
  656.0 41.6 all-gather.5
  718.1 53.4 reduce-scatter.1
  785.0 41.5 all-gather.5
  847.0 53.4 reduce-scatter.1
  913.6 41.6 all-gather.5
  975.7 53.4 reduce-scatter.1
  1042.3 41.6 all-gather.5
  1104.3 53.4 reduce-scatter.1
Sparse Core Ops, SparseCore 1:
  1170.3 40.4 all-gather.3
where the time goes:
time: 1230 us; the launch traced here: 1220 us
  waiting for transfers between devices  945 us (77%)
  matrix products  126 us (10%)
  other arithmetic  71.4 us (6%)
  starting transfers between devices  32.8 us (3%)
  local copies, waits for them, and re-layouts  27.5 us (2%)
  between operations  15.5 us (1%)
    reduce_scatter x9, waiting for transfers between devices, tick(): lax.psum_scatter(partial_value.astype(jnp.bfloat16), 'tp', scatter_dimens...  481 us
    all_gather x9, waiting for transfers between devices, tick(): features = lax.all_gather(layer_in, 'tp', axis=1, tiled=True)  359 us
    dot_general x9, matrix products, tick(): jnp.dot(normed, query_weight, preferred_element_type=jnp.float32)  55.6 us
    ppermute x9, waiting for transfers between devices, shifted(): return lax.ppermute(block, axis, route)  53.8 us
    all_gather x1, waiting for transfers between devices, shards(): gathered = lax.all_gather(pieces[None], 'tp', axis=0, tiled=True)  41.6 us
    ppermute x9, starting transfers between devices, shifted(): return lax.ppermute(block, axis, route)  28 us
  transfers between devices with their start and end apart: 38, of which 38 were waited for; matrix products, arithmetic and copies ran while one was open for 2% of the time, Pallas kernels for 0%

commit v1 on v0

v1 whole, which is shorter than its diff:
```python
import functools
import math

import jax
import jax.numpy as jnp
from jax import lax
from jax.experimental import pallas as pl
from jax.experimental.pallas import tpu as pltpu
from jax.sharding import Mesh
from jax.sharding import PartitionSpec as P

HD = 128
SLOTS = 2
EPS = 1e-05
ROWS = 64
LIMIT = 16 * 2**20


def swap(x):
    return lax.ppermute(x, "core", [(0, 1), (1, 0)])


def by_core(core, mine, other, axis):
    return jnp.where(
        core == 0,
        jnp.concatenate([mine, other], axis),
        jnp.concatenate([other, mine], axis),
    )


def exchange(blocks):
    flat = blocks.reshape(blocks.shape[0] * blocks.shape[1], blocks.shape[2])
    moved = lax.all_to_all(flat, "chip", split_axis=0, concat_axis=0, tiled=True)
    return moved.reshape(blocks.shape)


def dot(a, b):
    return jnp.dot(a, b, preferred_element_type=jnp.float32)


def turn(values, cosine, sine):
    return values * cosine + pltpu.roll(values, HD // 2, 1) * sine


def project_kernel(x_ref, gain_ref, mine_ref, other_ref, pair_ref, keep_ref, give_ref):
    n_chip, rows, width = x_ref.shape
    columns = mine_ref.shape[1]
    square = jnp.zeros((rows, 1), jnp.float32)
    parts = []
    for j in range(n_chip):
        part = x_ref[j].astype(jnp.float32)
        square += jnp.sum(part * part, axis=-1, keepdims=True)
        parts.append((part * gain_ref[j : j + 1, :]).astype(jnp.bfloat16))
    scaled = jnp.concatenate(parts, axis=1)
    keep_ref[:, :columns] = dot(scaled, mine_ref[...])
    give_ref[:, :columns] = dot(scaled, other_ref[...])
    pair = dot(scaled, pair_ref[...])
    squares = jnp.broadcast_to(square, (rows, HD))
    for ref in (keep_ref, give_ref):
        ref[:, columns : columns + 2 * HD] = pair
        ref[:, columns + 2 * HD :] = squares


def attend_kernel(
    depth, where_ref, keep_ref, got_ref, cos_ref, sin_ref, held_ref, fresh_ref, attended_ref, new_ref
):
    rows, columns = attended_ref.shape
    batch, length, offset, valid = where_ref[0], where_ref[1], where_ref[2], where_ref[3]
    cached = held_ref.shape[1]
    span = fresh_ref.shape[1]
    total = keep_ref[...] + got_ref[...]
    square = total[:, columns + 2 * HD : columns + 2 * HD + 1]
    scale = lax.rsqrt(square / depth + EPS)
    cosine = cos_ref[...] * scale
    sine = sin_ref[...] * scale
    pair = total[:, columns : columns + 2 * HD]
    low = HD // 2
    keys = jnp.concatenate([pair[:, :low], pair[:, HD : HD + low]], axis=1)
    values = jnp.concatenate([pair[:, low:HD], pair[:, HD + low :]], axis=1) * scale
    new_ref[...] = fresh_ref[...]

    @pl.when(valid == 1)
    def _():
        place = pl.ds(pl.multiple_of(offset, rows), rows)
        new_ref[batch, place, :HD] = turn(keys, cosine, sine).astype(jnp.bfloat16)
        new_ref[batch, place, HD:] = values.astype(jnp.bfloat16)

    live = lax.broadcasted_iota(jnp.int32, (1, cached), 1) < length
    row = lax.broadcasted_iota(jnp.int32, (rows, span), 0) + offset
    causal = lax.broadcasted_iota(jnp.int32, (rows, span), 1) <= row
    heads = columns // HD
    group = max(1, min(heads, 128 // rows))
    causal = jnp.concatenate([causal] * group, axis=0)
    root = 1.0 / math.sqrt(HD)
    contract = (((1,), (1,)), ((), ()))
    for base in range(0, heads, group):
        queries = jnp.concatenate(
            [
                turn(total[:, h * HD : (h + 1) * HD], cosine, sine).astype(jnp.bfloat16)
                for h in range(base, base + group)
            ],
            axis=0,
        )
        scores = lax.dot_general(
            queries, held_ref[batch, :, :HD], contract, preferred_element_type=jnp.float32
        )
        scores = jnp.where(live, scores, -1e30)
        recent = lax.dot_general(
            queries, new_ref[batch, :, :HD], contract, preferred_element_type=jnp.float32
        )
        recent = jnp.where(causal, recent, -1e30)
        top = jnp.maximum(
            jnp.max(scores, axis=-1, keepdims=True), jnp.max(recent, axis=-1, keepdims=True)
        )
        scores = jnp.exp((scores - top) * root)
        recent = jnp.exp((recent - top) * root)
        weight = jnp.sum(scores, axis=-1, keepdims=True) + jnp.sum(recent, axis=-1, keepdims=True)
        mixed = dot(scores.astype(jnp.bfloat16), held_ref[batch, :, HD:]) + dot(
            recent.astype(jnp.bfloat16), new_ref[batch, :, HD:]
        )
        mixed = (mixed / weight).astype(jnp.bfloat16)
        for h in range(group):
            attended_ref[:, (base + h) * HD : (base + h + 1) * HD] = mixed[
                h * rows : (h + 1) * rows
            ]


def out_kernel(mine_ref, got_ref, own_ref, other_ref, partial_ref):
    n_chip, _, width = partial_ref.shape
    for j in range(n_chip):
        columns = slice(j * width, (j + 1) * width)
        partial = dot(mine_ref[...], own_ref[:, columns]) + dot(got_ref[...], other_ref[:, columns])
        partial_ref[j] = partial.astype(jnp.bfloat16)


def fast(x):
    return pltpu.with_memory_space_constraint(x, pltpu.VMEM)


def call(kernel, out, flops, scalars, arrays):
    return pl.pallas_call(
        kernel,
        out_shape=out,
        in_specs=[pl.BlockSpec(memory_space=pltpu.SMEM)] * scalars
        + [pl.BlockSpec(memory_space=pltpu.VMEM)] * arrays,
        out_specs=jax.tree.map(lambda _: pl.BlockSpec(memory_space=pltpu.VMEM), out),
        compiler_params=pltpu.CompilerParams(vmem_limit_bytes=LIMIT),
        cost_estimate=pl.CostEstimate(flops=flops, bytes_accessed=2**20, transcendentals=0),
    )


def shards(hidden_in, norm_gain, w_query, w_key_value, w_out, cache, ctx_len, placement):
    n_section = lax.axis_size("section")
    n_chip = lax.axis_size("chip")
    section = lax.axis_index("section")
    chip = lax.axis_index("chip")
    core = lax.axis_index("core")
    micro, span, width = hidden_in.shape
    rows = min(ROWS, span)
    parts = span // rows
    chunks = micro * parts
    steps = n_section + chunks - 1
    depth = n_chip * 2 * width
    columns = w_query.shape[2]
    bf16 = jnp.bfloat16
    inputs = hidden_in.reshape(chunks, rows, width)

    def halves(x, axis):
        keep = lax.dynamic_index_in_dim(x, core, axis, keepdims=False)
        give = lax.dynamic_index_in_dim(x, 1 - core, axis, keepdims=False)
        return keep, swap(give)

    wq_own, wq_other = halves(w_query[0].reshape(n_chip, 2, width, columns), 1)
    pair_own, pair_other = halves(w_key_value[0].reshape(n_chip, 2, width, HD), 1)
    wq_own = wq_own.reshape(depth // 2, columns)
    wq_other = wq_other.reshape(depth // 2, columns)
    w_pair = by_core(core, pair_own, pair_other, 2).reshape(depth // 2, 2 * HD)
    gain = lax.dynamic_index_in_dim(norm_gain[0].reshape(n_chip, 2, width), core, 1, keepdims=False)
    context = by_core(core, cache[0], swap(cache[0]), 1)
    wo_own, wo_other = halves(w_out[0].reshape(columns, n_chip, 2, width), 2)
    wo_own = wo_own.reshape(columns, depth // 2)
    wo_other = wo_other.reshape(columns, depth // 2)

    freqs = jnp.exp(jnp.arange(HD // 2, dtype=jnp.float32) * (-2.0 * math.log(500000.0) / HD))
    order = jnp.clip(jnp.arange(steps) - section, 0, chunks - 1)
    batches = order // parts
    offsets = (order % parts) * rows
    valids = (jnp.arange(steps) >= section) & (jnp.arange(steps) < section + chunks)
    wheres = jnp.stack(
        [batches, ctx_len[batches], offsets, valids.astype(jnp.int32)], axis=1
    ).astype(jnp.int32)
    chunk = jnp.arange(chunks)
    positions = (ctx_len[chunk // parts] + (chunk % parts) * rows)[:, None] + jnp.arange(
        rows, dtype=jnp.int32
    )
    angles = positions.astype(jnp.float32)[:, :, None] * freqs
    cosines = jnp.concatenate([jnp.cos(angles), jnp.cos(angles)], axis=-1)
    sines = jnp.concatenate([-jnp.sin(angles), jnp.sin(angles)], axis=-1)
    wq_own, wq_other, wo_own, wo_other, w_pair, context = (
        fast(v) for v in (wq_own, wq_other, wo_own, wo_other, w_pair, context)
    )
    packed = jax.ShapeDtypeStruct((rows, columns + 3 * HD), jnp.float32)
    project = call(
        project_kernel, (packed, packed), rows * depth * 2 * (columns + HD), 0, 5
    )
    attend = call(
        functools.partial(attend_kernel, depth),
        (
            jax.ShapeDtypeStruct((rows, columns), bf16),
            jax.ShapeDtypeStruct((micro, span, 2 * HD), bf16),
        ),
        4 * rows * columns * (context.shape[1] + span),
        1,
        6,
    )
    finish = call(
        out_kernel,
        jax.ShapeDtypeStruct((n_chip, rows, width), bf16),
        2 * rows * columns * depth,
        0,
        4,
    )

    incoming = None
    fresh = jnp.zeros((micro, span, 2 * HD), bf16)
    updates = []
    for step in range(steps):
        if step < chunks:
            layer_in = inputs[step]
            if step > 0:
                layer_in = jnp.where(section == 0, layer_in, incoming)
        else:
            layer_in = incoming
        features = exchange(jnp.broadcast_to(layer_in[None], (n_chip, rows, width)))
        keep, give = project(features, gain, wq_own, wq_other, w_pair)
        cosine = lax.dynamic_index_in_dim(cosines, order[step], 0, keepdims=False)
        sine = lax.dynamic_index_in_dim(sines, order[step], 0, keepdims=False)
        attended, fresh = attend(
            wheres[step], keep, swap(give), cosine, sine, context, fresh
        )
        partial = finish(attended, swap(attended), wo_own, wo_other)
        pieces = exchange(partial).astype(jnp.float32)
        updated = (layer_in.astype(jnp.float32) + jnp.sum(pieces, axis=0)).astype(bf16)
        updates.append(updated)
        if step + 1 < steps:
            incoming = lax.ppermute(
                updated, "section", [(i, i + 1) for i in range(n_section - 1)]
            )
    outputs = lax.dynamic_slice_in_dim(jnp.stack(updates), section, chunks, 0)
    outputs = outputs.reshape(micro, span, width)

    half = span // 2
    here = lax.dynamic_slice_in_dim(fresh, core * half, half, 1).reshape(1, micro * half, 2 * HD)
    blocks = exchange(jnp.broadcast_to(here, (n_chip, micro * half, 2 * HD)))
    blocks = blocks.reshape(n_chip * micro, half, 2 * HD)
    holders = placement[0].reshape(-1)
    count = holders.shape[0]
    earlier = (holders[None, :] == holders[:, None]) & (
        jnp.arange(count)[None, :] < jnp.arange(count)[:, None]
    )
    ranks = jnp.sum(earlier.astype(jnp.int32), axis=-1)

    def pick(member):
        chosen = (holders[None, :] == member) & (ranks[None, :] == jnp.arange(SLOTS)[:, None])
        found = jnp.any(chosen, axis=1)
        which = jnp.sum(chosen.astype(jnp.int32) * jnp.arange(count)[None, :], axis=1)
        return jnp.stack(
            [
                jnp.where(
                    found[s], lax.dynamic_index_in_dim(blocks, which[s], 0, keepdims=False), 0
                )
                for s in range(SLOTS)
            ]
        )

    store = by_core(core, pick(2 * chip + core), swap(pick(2 * chip + 1 - core)), 1)
    return (outputs[None], store[None])


def solution(mesh):
    n_section, n_tp = mesh.devices.shape
    fine = Mesh(mesh.devices.reshape(n_section, n_tp // 2, 2), ("section", "chip", "core"))
    tp = ("chip", "core")
    in_specs = (
        P(None, None, tp),
        P("section", None),
        P("section", None, tp),
        P("section", None, tp),
        P("section", tp, None),
        P("section", None, tp, None),
        P(),
        P("section", None, None),
    )
    out_specs = (P("section", None, None, tp), P("section", tp, None, None))
    return jax.shard_map(shards, mesh=fine, in_specs=in_specs, out_specs=out_specs, check_vma=False)
```

time: 1230 us -> 613 us (0.50)
  waiting for transfers between devices: 945 us -> 91.5 us
  blocking collectives: 0 us -> 207 us
  matrix products: 126 us -> 0 us
  Pallas kernels: 0 us -> 88.3 us
  starting transfers between devices: 32.8 us -> 89.2 us
  other arithmetic: 71.4 us -> 22.2 us
  local copies, waits for them, and re-layouts: 27.5 us -> 75.5 us
  between operations: 15.5 us -> 30 us
    reduce_scatter x9 -> x0, waiting for transfers between devices: 481 us -> none  [tick(): lax.psum_scatter(partial_value.astype(jnp.bfloat16), 'tp', scatter_dimens...]
    all_gather x10 -> x0, waiting for transfers between devices: 401 us -> none  [the longest x9 359 us: tick(): features = lax.all_gather(layer_in, 'tp', axis=1, tiled=True)]
    all_to_all x0 -> x19, blocking collectives: none -> 207 us  [exchange(): lax.all_to_all(flat, 'chip', split_axis=0, concat_axis=0, tiled=True)]
    dot_general x64 -> x0, matrix products: 126 us -> none  [the longest x9 55.6 us: tick(): jnp.dot(normed, query_weight, preferred_element_type=jnp.float32)]
    pallas_call x0 -> x33, Pallas kernels: none -> 88.3 us  [the longest x11 45.6 us: shards(): keep, give = project(features, gain, wq_own, wq_other, w_pair)]
    ppermute x19 -> x37, starting transfers between devices: 32 us -> 69.3 us  [the longest x27 49 us: swap(): return lax.ppermute(x, 'core', [(0, 1), (1, 0)])]
    unnamed x6 -> x67, local copies, waits for them, and re-layouts: 0.76 us -> 36.3 us
    reduce_sum x27 -> x12, other arithmetic: 28.6 us -> 0.91 us  [the longest x11 0.77 us: shards(): jnp.sum(pieces, axis=0)]
  transfers between devices with their start and end apart: 38 -> 41, of which waited for: 38 -> 30; matrix products, arithmetic and copies ran while one was open for 2% -> 10% of each run, Pallas kernels for 0% -> 1%
where the time goes in v1:
time: 613 us; the launch traced here: 604 us
  blocking collectives  207 us (34%)
  waiting for transfers between devices  91.5 us (15%)
  starting transfers between devices  89.2 us (15%)
  Pallas kernels  88.3 us (14%)
  local copies, waits for them, and re-layouts  75.5 us (12%)
  between operations  30 us (5%)
  other arithmetic  22.2 us (4%)
    all_to_all x19, blocking collectives, exchange(): lax.all_to_all(flat, 'chip', split_axis=0, concat_axis=0, tiled=True)  207 us
    ppermute x10, waiting for transfers between devices, shards(): lax.ppermute(updated, 'section', [(i, i + 1) for i in range(n_section - 1)])  66.7 us
    ppermute x27, starting transfers between devices, swap(): return lax.ppermute(x, 'core', [(0, 1), (1, 0)])  49 us
    pallas_call x11, Pallas kernels, shards(): keep, give = project(features, gain, wq_own, wq_other, w_pair)  45.6 us
    unnamed x67, local copies, waits for them, and re-layouts  36.3 us
    pallas_call x11, Pallas kernels, shards(): attend(wheres[step], keep, swap(give), cosine, sine, context, fresh)  24 us
    ppermute x10, starting transfers between devices, shards(): lax.ppermute(updated, 'section', [(i, i + 1) for i in range(n_section - 1)])  20.3 us
    all_to_all x4, starting transfers between devices, exchange(): lax.all_to_all(flat, 'chip', split_axis=0, concat_axis=0, tiled=True)  19.9 us
  transfers between devices with their start and end apart: 41, of which 30 were waited for; matrix products, arithmetic and copies ran while one was open for 10% of the time, Pallas kernels for 1%

profile of v1, /device:TPU:73, one launch (start us, length us, event | category | flops | bytes accessed | tf_op | source)
XLA Modules:
  0.0 603.5 jit_solution(15525916185193218996)
XLA Ops:
  0.6 7.4 %dynamic-slice_bitcast_fusion = (bf16[8,512,512]{2,1,0:T(8,128)(2,1)}, bf16[8,1,512,512]{3,2,1,0:T(8,128)(2,1)}) fusion(bf16[8,2,512,512]{3,2,1,0:T(8,128)(2,1)} %bitcast.176, s32[]{:T(128)S(6)} %select_n.233, s32[]{:T(128)S(6)} %select_n.232), kind=kLoop, calls=%fused_computation.1 | loop fusion | bytes 16777224 | tf_op jit(solution)/shard_map/jit(dynamic_index_in_dim)/squeeze | solution.py:170
  8.7 12.0 %copy.43 = bf16[1,512,8192]{1,2,0:T(8,128)(2,1)} copy(bf16[1,512,8192]{2,1,0:T(8,128)(2,1)} %param.12) | data formatting | bytes 16777216 | tf_op args[4]
  20.7 7.5 %constant_dynamic-slice_fusion.2 = (bf16[512,8,1,512]{0,3,2,1:T(8,128)(2,1)}, bf16[512,8,1,512]{0,3,2,1:T(8,128)(2,1)}) fusion(bf16[512,8,2,512]{0,3,2,1:T(8,128)(2,1)} %bitcast.174, s32[]{:T(128)S(6)} %select_n.233, s32[]{:T(128)S(6)} %select_n.232), kind=kLoop, calls=%fused_computation.149 | loop fusion | bytes 16777224 | tf_op jit(solution)/shard_map/jit(dynamic_index_in_dim)/dynamic_slice | solution.py:170
  28.2 8.2 %copy.45 = bf16[512,8,1,512]{3,1,0,2:T(8,128)(2,1)} copy(bf16[512,8,1,512]{0,3,2,1:T(8,128)(2,1)} %get-tuple-element.123) | data formatting | bytes 8388608 | tf_op jit(solution)/shard_map/jit(dynamic_index_in_dim)/dynamic_slice | solution.py:170
  98.0 12.6 %all_to_all.138 = bf16[8,64,512]{2,1,0:T(8,128)(2,1)S(1)} all-to-all(bf16[8,64,512]{2,1,0:T(8,128)(2,1)S(1)} %shard_map.97), channel_id=1, replica_groups=mesh['section'=8,'chip'=8,'core'=2] {'chip'}, dimensions={0} | all-to-all | bytes 1048576 | tf_op jit(solution)/shard_map/all_to_all | solution.py:33
  119.4 10.2 %all_to_all.139.x_ref = bf16[8,64,512]{2,1,0:T(8,128)(2,1)S(1)} all-to-all(bf16[8,64,512]{2,1,0:T(8,128)(2,1)S(1)} %broadcast_in_dim.39), channel_id=1, replica_groups=mesh['section'=8,'chip'=8,'core'=2] {'chip'}, dimensions={0} | all-to-all | bytes 1048576 | tf_op jit(solution)/shard_map/all_to_all | solution.py:33
  164.0 7.4 %collective-permute-done.9 = bf16[64,512]{1,0:T(8,128)(2,1)S(1)} collective-permute-done((bf16[64,512]{1,0:T(8,128)(2,1)S(1)}, bf16[64,512]{1,0:T(8,128)(2,1)S(1)}, u32[]{:S(2)}, u32[]{:S(2)}) %collective-permute-start.9) | collective-permute-done | bytes 65568 | tf_op jit(solution)/shard_map/ppermute | solution.py:246
  172.3 9.8 %all_to_all.140.x_ref = bf16[8,64,512]{2,1,0:T(8,128)(2,1)S(1)} all-to-all(bf16[8,64,512]{2,1,0:T(8,128)(2,1)S(1)} %broadcast_in_dim.40), channel_id=1, replica_groups=mesh['section'=8,'chip'=8,'core'=2] {'chip'}, dimensions={0} | all-to-all | bytes 1048576 | tf_op jit(solution)/shard_map/all_to_all | solution.py:33
  206.3 12.1 %all_to_all.141 = bf16[8,64,512]{2,1,0:T(8,128)(2,1)S(1)} all-to-all(bf16[8,64,512]{2,1,0:T(8,128)(2,1)S(1)} %shard_map.103), channel_id=1, replica_groups=mesh['section'=8,'chip'=8,'core'=2] {'chip'}, dimensions={0} | all-to-all | bytes 1048576 | tf_op jit(solution)/shard_map/all_to_all | solution.py:33
  221.1 6.9 %collective-permute-done.12 = bf16[64,512]{1,0:T(8,128)(2,1)S(1)} collective-permute-done((bf16[64,512]{1,0:T(8,128)(2,1)S(1)}, bf16[64,512]{1,0:T(8,128)(2,1)S(1)}, u32[]{:S(2)}, u32[]{:S(2)}) %collective-permute-start.12) | collective-permute-done | bytes 65568 | tf_op jit(solution)/shard_map/ppermute | solution.py:246
  228.9 10.3 %all_to_all.142.x_ref = bf16[8,64,512]{2,1,0:T(8,128)(2,1)S(1)} all-to-all(bf16[8,64,512]{2,1,0:T(8,128)(2,1)S(1)} %broadcast_in_dim.41), channel_id=1, replica_groups=mesh['section'=8,'chip'=8,'core'=2] {'chip'}, dimensions={0} | all-to-all | bytes 1048576 | tf_op jit(solution)/shard_map/all_to_all | solution.py:33
  253.4 11.7 %all_to_all.143 = bf16[8,64,512]{2,1,0:T(8,128)(2,1)S(1)} all-to-all(bf16[8,64,512]{2,1,0:T(8,128)(2,1)S(1)} %shard_map.106), channel_id=1, replica_groups=mesh['section'=8,'chip'=8,'core'=2] {'chip'}, dimensions={0} | all-to-all | bytes 1048576 | tf_op jit(solution)/shard_map/all_to_all | solution.py:33
  267.8 6.7 %collective-permute-done.15 = bf16[64,512]{1,0:T(8,128)(2,1)S(1)} collective-permute-done((bf16[64,512]{1,0:T(8,128)(2,1)S(1)}, bf16[64,512]{1,0:T(8,128)(2,1)S(1)}, u32[]{:S(2)}, u32[]{:S(2)}) %collective-permute-start.15) | collective-permute-done | bytes 65568 | tf_op jit(solution)/shard_map/ppermute | solution.py:246
  274.5 10.0 %all_to_all.144.x_ref = bf16[8,64,512]{2,1,0:T(8,128)(2,1)S(1)} all-to-all(bf16[8,64,512]{2,1,0:T(8,128)(2,1)S(1)} %broadcast_in_dim.42), channel_id=1, replica_groups=mesh['section'=8,'chip'=8,'core'=2] {'chip'}, dimensions={0} | all-to-all | bytes 1048576 | tf_op jit(solution)/shard_map/all_to_all | solution.py:33
  299.1 11.5 %all_to_all.145 = bf16[8,64,512]{2,1,0:T(8,128)(2,1)S(1)} all-to-all(bf16[8,64,512]{2,1,0:T(8,128)(2,1)S(1)} %shard_map.109), channel_id=1, replica_groups=mesh['section'=8,'chip'=8,'core'=2] {'chip'}, dimensions={0} | all-to-all | bytes 1048576 | tf_op jit(solution)/shard_map/all_to_all | solution.py:33
  313.2 6.7 %collective-permute-done.18 = bf16[64,512]{1,0:T(8,128)(2,1)S(1)} collective-permute-done((bf16[64,512]{1,0:T(8,128)(2,1)S(1)}, bf16[64,512]{1,0:T(8,128)(2,1)S(1)}, u32[]{:S(2)}, u32[]{:S(2)}) %collective-permute-start.18) | collective-permute-done | bytes 65568 | tf_op jit(solution)/shard_map/ppermute | solution.py:246
  320.0 10.1 %all_to_all.146.x_ref = bf16[8,64,512]{2,1,0:T(8,128)(2,1)S(1)} all-to-all(bf16[8,64,512]{2,1,0:T(8,128)(2,1)S(1)} %broadcast_in_dim.43), channel_id=1, replica_groups=mesh['section'=8,'chip'=8,'core'=2] {'chip'}, dimensions={0} | all-to-all | bytes 1048576 | tf_op jit(solution)/shard_map/all_to_all | solution.py:33
  344.6 11.5 %all_to_all.147 = bf16[8,64,512]{2,1,0:T(8,128)(2,1)S(1)} all-to-all(bf16[8,64,512]{2,1,0:T(8,128)(2,1)S(1)} %shard_map.112), channel_id=1, replica_groups=mesh['section'=8,'chip'=8,'core'=2] {'chip'}, dimensions={0} | all-to-all | bytes 1048576 | tf_op jit(solution)/shard_map/all_to_all | solution.py:33
  358.7 6.7 %collective-permute-done.21 = bf16[64,512]{1,0:T(8,128)(2,1)S(1)} collective-permute-done((bf16[64,512]{1,0:T(8,128)(2,1)S(1)}, bf16[64,512]{1,0:T(8,128)(2,1)S(1)}, u32[]{:S(2)}, u32[]{:S(2)}) %collective-permute-start.21) | collective-permute-done | bytes 65568 | tf_op jit(solution)/shard_map/ppermute | solution.py:246
  365.5 10.1 %all_to_all.148.x_ref = bf16[8,64,512]{2,1,0:T(8,128)(2,1)S(1)} all-to-all(bf16[8,64,512]{2,1,0:T(8,128)(2,1)S(1)} %broadcast_in_dim.44), channel_id=1, replica_groups=mesh['section'=8,'chip'=8,'core'=2] {'chip'}, dimensions={0} | all-to-all | bytes 1048576 | tf_op jit(solution)/shard_map/all_to_all | solution.py:33
  390.0 11.5 %all_to_all.149 = bf16[8,64,512]{2,1,0:T(8,128)(2,1)S(1)} all-to-all(bf16[8,64,512]{2,1,0:T(8,128)(2,1)S(1)} %shard_map.115), channel_id=1, replica_groups=mesh['section'=8,'chip'=8,'core'=2] {'chip'}, dimensions={0} | all-to-all | bytes 1048576 | tf_op jit(solution)/shard_map/all_to_all | solution.py:33
  404.2 6.7 %collective-permute-done.24 = bf16[64,512]{1,0:T(8,128)(2,1)S(1)} collective-permute-done((bf16[64,512]{1,0:T(8,128)(2,1)S(1)}, bf16[64,512]{1,0:T(8,128)(2,1)S(1)}, u32[]{:S(2)}, u32[]{:S(2)}) %collective-permute-start.24) | collective-permute-done | bytes 65568 | tf_op jit(solution)/shard_map/ppermute | solution.py:246
  410.9 10.3 %all_to_all.150.x_ref = bf16[8,64,512]{2,1,0:T(8,128)(2,1)S(1)} all-to-all(bf16[8,64,512]{2,1,0:T(8,128)(2,1)S(1)} %broadcast_in_dim.45), channel_id=1, replica_groups=mesh['section'=8,'chip'=8,'core'=2] {'chip'}, dimensions={0} | all-to-all | bytes 1048576 | tf_op jit(solution)/shard_map/all_to_all | solution.py:33
  435.7 11.5 %all_to_all.151 = bf16[8,64,512]{2,1,0:T(8,128)(2,1)S(1)} all-to-all(bf16[8,64,512]{2,1,0:T(8,128)(2,1)S(1)} %shard_map.118), channel_id=1, replica_groups=mesh['section'=8,'chip'=8,'core'=2] {'chip'}, dimensions={0} | all-to-all | bytes 1048576 | tf_op jit(solution)/shard_map/all_to_all | solution.py:33
  449.8 6.7 %collective-permute-done.27 = bf16[64,512]{1,0:T(8,128)(2,1)S(1)} collective-permute-done((bf16[64,512]{1,0:T(8,128)(2,1)S(1)}, bf16[64,512]{1,0:T(8,128)(2,1)S(1)}, u32[]{:S(2)}, u32[]{:S(2)}) %collective-permute-start.27) | collective-permute-done | bytes 65568 | tf_op jit(solution)/shard_map/ppermute | solution.py:246
  456.5 10.1 %all_to_all.152.x_ref = bf16[8,64,512]{2,1,0:T(8,128)(2,1)S(1)} all-to-all(bf16[8,64,512]{2,1,0:T(8,128)(2,1)S(1)} %broadcast_in_dim.46), channel_id=1, replica_groups=mesh['section'=8,'chip'=8,'core'=2] {'chip'}, dimensions={0} | all-to-all | bytes 1048576 | tf_op jit(solution)/shard_map/all_to_all | solution.py:33
  481.0 11.5 %all_to_all.153 = bf16[8,64,512]{2,1,0:T(8,128)(2,1)S(1)} all-to-all(bf16[8,64,512]{2,1,0:T(8,128)(2,1)S(1)} %shard_map.121), channel_id=1, replica_groups=mesh['section'=8,'chip'=8,'core'=2] {'chip'}, dimensions={0} | all-to-all | bytes 1048576 | tf_op jit(solution)/shard_map/all_to_all | solution.py:33
  495.2 6.7 %collective-permute-done.30 = bf16[64,512]{1,0:T(8,128)(2,1)S(1)} collective-permute-done((bf16[64,512]{1,0:T(8,128)(2,1)S(1)}, bf16[64,512]{1,0:T(8,128)(2,1)S(1)}, u32[]{:S(2)}, u32[]{:S(2)}) %collective-permute-start.30) | collective-permute-done | bytes 65568 | tf_op jit(solution)/shard_map/ppermute | solution.py:246
  501.9 10.1 %all_to_all.154.x_ref = bf16[8,64,512]{2,1,0:T(8,128)(2,1)S(1)} all-to-all(bf16[8,64,512]{2,1,0:T(8,128)(2,1)S(1)} %broadcast_in_dim.47), channel_id=1, replica_groups=mesh['section'=8,'chip'=8,'core'=2] {'chip'}, dimensions={0} | all-to-all | bytes 1048576 | tf_op jit(solution)/shard_map/all_to_all | solution.py:33
  526.6 11.5 %all_to_all.155 = bf16[8,64,512]{2,1,0:T(8,128)(2,1)S(1)} all-to-all(bf16[8,64,512]{2,1,0:T(8,128)(2,1)S(1)} %shard_map.124), channel_id=1, replica_groups=mesh['section'=8,'chip'=8,'core'=2] {'chip'}, dimensions={0} | all-to-all | bytes 1048576 | tf_op jit(solution)/shard_map/all_to_all | solution.py:33
  540.8 6.7 %collective-permute-done.33 = bf16[64,512]{1,0:T(8,128)(2,1)S(1)} collective-permute-done((bf16[64,512]{1,0:T(8,128)(2,1)S(1)}, bf16[64,512]{1,0:T(8,128)(2,1)S(1)}, u32[]{:S(2)}, u32[]{:S(2)}) %collective-permute-start.33) | collective-permute-done | bytes 65568 | tf_op jit(solution)/shard_map/ppermute | solution.py:246
  547.5 10.1 %all_to_all.156.x_ref = bf16[8,64,512]{2,1,0:T(8,128)(2,1)S(1)} all-to-all(bf16[8,64,512]{2,1,0:T(8,128)(2,1)S(1)} %broadcast_in_dim.48), channel_id=1, replica_groups=mesh['section'=8,'chip'=8,'core'=2] {'chip'}, dimensions={0} | all-to-all | bytes 1048576 | tf_op jit(solution)/shard_map/all_to_all | solution.py:33
  (251 shorter events, 270.5 us)
Async XLA Ops:
  8.0 64.5 %collective-permute-start = (bf16[8,512,512]{2,1,0:T(8,128)(2,1)}, bf16[8,512,512]{2,1,0:T(8,128)(2,1)}, u32[]{:S(2)}, u32[]{:S(2)}) collective-permute-start(bf16[8,512,512]{2,1,0:T(8,128)(2,1)} %get-tuple-element.125), channel_id=1, source_target_pairs={{0,1},{1,0},{2,3},{3,2},{4,5},{5,4},{6,7},{7,6},{8,9},{9,8},{10,11... | collective-permute-start | bytes 12582920 | tf_op jit(solution)/shard_map/ppermute | solution.py:20
  36.4 54.9 %collective-permute-start.5 = (bf16[512,8,512]{2,1,0:T(8,128)(2,1)}, bf16[512,8,512]{2,1,0:T(8,128)(2,1)}, u32[]{:S(2)}, u32[]{:S(2)}) collective-permute-start(bf16[512,8,512]{2,1,0:T(8,128)(2,1)} %bitcast.178), channel_id=1, source_target_pairs={{0,1},{1,0},{2,3},{3,2},{4,5},{5,4},{6,7},{7,6},{8,9},{9,8},{10,11... | collective-permute-start | bytes 12582920 | tf_op jit(solution)/shard_map/ppermute | solution.py:20
  38.1 34.4 %all-to-all-start = ((bf16[8,64,512]{2,1,0:T(8,128)(2,1)}), bf16[8,64,512]{2,1,0:T(8,128)(2,1)S(1)}, u32[]{:S(2)}, u32[]{:S(2)}) async-start(bf16[8,64,512]{2,1,0:T(8,128)(2,1)} %broadcast_in_dim.37), calls=%async_computation | async-start | bytes 1048576 | tf_op jit(solution)/shard_map/all_to_all | solution.py:33
  43.5 36.8 %collective-permute-start.3 = (bf16[2,1024,256]{2,1,0:T(8,128)(2,1)}, bf16[2,1024,256]{2,1,0:T(8,128)(2,1)}, u32[]{:S(2)}, u32[]{:S(2)}) collective-permute-start(bf16[2,1024,256]{2,1,0:T(8,128)(2,1)} %bitcast.180), channel_id=1, source_target_pairs={{0,1},{1,0},{2,3},{3,2},{4,5},{5,4},{6,7},{7,6},{8,9},{9,8},{10,11... | collective-permute-start | bytes 3145736 | tf_op jit(solution)/shard_map/ppermute | solution.py:20
  46.0 22.7 %collective-permute-start.1 = (bf16[8,512,128]{2,1,0:T(8,128)(2,1)}, bf16[8,512,128]{2,1,0:T(8,128)(2,1)S(1)}, u32[]{:S(2)}, u32[]{:S(2)}) collective-permute-start(bf16[8,512,128]{2,1,0:T(8,128)(2,1)} %get-tuple-element.128), channel_id=1, source_target_pairs={{0,1},{1,0},{2,3},{3,2},{4,5},{5,4},{6,7},{7,6},{8,9},{9,8},{10,11... | collective-permute-start | bytes 3145736 | tf_op jit(solution)/shard_map/ppermute | solution.py:20
  79.7 2.8 collective-permute-start.2
  84.6 11.4 %collective-permute-start.4 = (bf16[64,512]{1,0:T(8,128)(2,1)S(1)}, bf16[64,512]{1,0:T(8,128)(2,1)S(1)}, u32[]{:S(2)}, u32[]{:S(2)}) collective-permute-start(bf16[64,512]{1,0:T(8,128)(2,1)S(1)} %get-tuple-element.48.mine_ref), channel_id=1, source_target_pairs={{0,1},{1,0},{2,3},{3,2},{4,5},{5,4},{6,7},{7,6},{8,9},{9,8},{10,11... | collective-permute-start | bytes 196616 | tf_op jit(solution)/shard_map/ppermute | solution.py:20
  110.7 8.6 %collective-permute-start.6 = (bf16[64,512]{1,0:T(8,128)(2,1)S(1)}, bf16[64,512]{1,0:T(8,128)(2,1)S(1)}, u32[]{:S(2)}, u32[]{:S(2)}) collective-permute-start(bf16[64,512]{1,0:T(8,128)(2,1)S(1)} %add_convert_fusion.10), channel_id=1, source_target_pairs={{0,16},{16,32},{32,48},{48,64},{64,80},{80,96},{96,112},{1,17},{17... | collective-permute-start | bytes 196616 | tf_op jit(solution)/shard_map/ppermute | solution.py:246
  137.6 5.2 collective-permute-start.7
  148.7 12.7 %all-to-all-start.3 = ((bf16[8,64,512]{2,1,0:T(8,128)(2,1)}), bf16[8,64,512]{2,1,0:T(8,128)(2,1)S(1)}, u32[]{:S(2)}, u32[]{:S(2)}) async-start(bf16[8,64,512]{2,1,0:T(8,128)(2,1)} %shard_map.100), calls=%async_computation.3 | async-start | bytes 1048576 | tf_op jit(solution)/shard_map/all_to_all | solution.py:33
  162.1 9.3 %collective-permute-start.9 = (bf16[64,512]{1,0:T(8,128)(2,1)S(1)}, bf16[64,512]{1,0:T(8,128)(2,1)S(1)}, u32[]{:S(2)}, u32[]{:S(2)}) collective-permute-start(bf16[64,512]{1,0:T(8,128)(2,1)S(1)} %get-tuple-element.122), channel_id=1, source_target_pairs={{0,16},{16,32},{32,48},{48,64},{64,80},{80,96},{96,112},{1,17},{17... | collective-permute-start | bytes 196616 | tf_op jit(solution)/shard_map/ppermute | solution.py:246
  188.4 8.2 %collective-permute-start.10 = (f32[64,896]{1,0:T(8,128)S(1)}, f32[64,896]{1,0:T(8,128)S(1)}, u32[]{:S(2)}, u32[]{:S(2)}) collective-permute-start(f32[64,896]{1,0:T(8,128)S(1)} %get-tuple-element.54), channel_id=1, source_target_pairs={{0,1},{1,0},{2,3},{3,2},{4,5},{5,4},{6,7},{7,6},{8,9},{9,8},{10,11... | collective-permute-start | bytes 688136 | tf_op jit(solution)/shard_map/ppermute | solution.py:20
  219.2 8.8 %collective-permute-start.12 = (bf16[64,512]{1,0:T(8,128)(2,1)S(1)}, bf16[64,512]{1,0:T(8,128)(2,1)S(1)}, u32[]{:S(2)}, u32[]{:S(2)}) collective-permute-start(bf16[64,512]{1,0:T(8,128)(2,1)S(1)} %get-tuple-element.120), channel_id=1, source_target_pairs={{0,16},{16,32},{32,48},{48,64},{64,80},{80,96},{96,112},{1,17},{17... | collective-permute-start | bytes 196616 | tf_op jit(solution)/shard_map/ppermute | solution.py:246
  243.5 4.9 collective-permute-start.13
  265.8 8.6 %collective-permute-start.15 = (bf16[64,512]{1,0:T(8,128)(2,1)S(1)}, bf16[64,512]{1,0:T(8,128)(2,1)S(1)}, u32[]{:S(2)}, u32[]{:S(2)}) collective-permute-start(bf16[64,512]{1,0:T(8,128)(2,1)S(1)} %get-tuple-element.118), channel_id=1, source_target_pairs={{0,16},{16,32},{32,48},{48,64},{64,80},{80,96},{96,112},{1,17},{17... | collective-permute-start | bytes 196616 | tf_op jit(solution)/shard_map/ppermute | solution.py:246
  288.6 5.2 collective-permute-start.16
  311.3 8.6 %collective-permute-start.18 = (bf16[64,512]{1,0:T(8,128)(2,1)S(1)}, bf16[64,512]{1,0:T(8,128)(2,1)S(1)}, u32[]{:S(2)}, u32[]{:S(2)}) collective-permute-start(bf16[64,512]{1,0:T(8,128)(2,1)S(1)} %get-tuple-element.116), channel_id=1, source_target_pairs={{0,16},{16,32},{32,48},{48,64},{64,80},{80,96},{96,112},{1,17},{17... | collective-permute-start | bytes 196616 | tf_op jit(solution)/shard_map/ppermute | solution.py:246
  334.3 5.2 collective-permute-start.19
  356.8 8.6 %collective-permute-start.21 = (bf16[64,512]{1,0:T(8,128)(2,1)S(1)}, bf16[64,512]{1,0:T(8,128)(2,1)S(1)}, u32[]{:S(2)}, u32[]{:S(2)}) collective-permute-start(bf16[64,512]{1,0:T(8,128)(2,1)S(1)} %get-tuple-element.114), channel_id=1, source_target_pairs={{0,16},{16,32},{32,48},{48,64},{64,80},{80,96},{96,112},{1,17},{17... | collective-permute-start | bytes 196616 | tf_op jit(solution)/shard_map/ppermute | solution.py:246
  379.7 5.2 collective-permute-start.22
  402.2 8.6 %collective-permute-start.24 = (bf16[64,512]{1,0:T(8,128)(2,1)S(1)}, bf16[64,512]{1,0:T(8,128)(2,1)S(1)}, u32[]{:S(2)}, u32[]{:S(2)}) collective-permute-start(bf16[64,512]{1,0:T(8,128)(2,1)S(1)} %get-tuple-element.112), channel_id=1, source_target_pairs={{0,16},{16,32},{32,48},{48,64},{64,80},{80,96},{96,112},{1,17},{17... | collective-permute-start | bytes 196616 | tf_op jit(solution)/shard_map/ppermute | solution.py:246
  425.4 5.2 collective-permute-start.25
  447.9 8.6 %collective-permute-start.27 = (bf16[64,512]{1,0:T(8,128)(2,1)S(1)}, bf16[64,512]{1,0:T(8,128)(2,1)S(1)}, u32[]{:S(2)}, u32[]{:S(2)}) collective-permute-start(bf16[64,512]{1,0:T(8,128)(2,1)S(1)} %get-tuple-element.110), channel_id=1, source_target_pairs={{0,16},{16,32},{32,48},{48,64},{64,80},{80,96},{96,112},{1,17},{17... | collective-permute-start | bytes 196616 | tf_op jit(solution)/shard_map/ppermute | solution.py:246
  470.8 5.2 collective-permute-start.28
  493.3 8.6 %collective-permute-start.30 = (bf16[64,512]{1,0:T(8,128)(2,1)S(1)}, bf16[64,512]{1,0:T(8,128)(2,1)S(1)}, u32[]{:S(2)}, u32[]{:S(2)}) collective-permute-start(bf16[64,512]{1,0:T(8,128)(2,1)S(1)} %get-tuple-element.108), channel_id=1, source_target_pairs={{0,16},{16,32},{32,48},{48,64},{64,80},{80,96},{96,112},{1,17},{17... | collective-permute-start | bytes 196616 | tf_op jit(solution)/shard_map/ppermute | solution.py:246
  516.2 5.2 collective-permute-start.31
  538.8 8.6 %collective-permute-start.33 = (bf16[64,512]{1,0:T(8,128)(2,1)S(1)}, bf16[64,512]{1,0:T(8,128)(2,1)S(1)}, u32[]{:S(2)}, u32[]{:S(2)}) collective-permute-start(bf16[64,512]{1,0:T(8,128)(2,1)S(1)} %get-tuple-element.106), channel_id=1, source_target_pairs={{0,16},{16,32},{32,48},{48,64},{64,80},{80,96},{96,112},{1,17},{17... | collective-permute-start | bytes 196616 | tf_op jit(solution)/shard_map/ppermute | solution.py:246
  561.8 5.2 collective-permute-start.34
  570.0 13.1 %all-to-all-start.22 = ((bf16[8,128,256]{2,1,0:T(8,128)(2,1)}), bf16[8,128,256]{2,1,0:T(8,128)(2,1)S(1)}, u32[]{:S(2)}, u32[]{:S(2)}) async-start(bf16[8,128,256]{2,1,0:T(8,128)(2,1)} %broadcast_in_dim.50), calls=%async_computation.22 | async-start | bytes 1048576 | tf_op jit(solution)/shard_map/all_to_all | solution.py:33
  574.7 1.6 collective-permute-start.35
  583.1 16.9 %all-to-all-start.21 = ((bf16[8,64,512]{2,1,0:T(8,128)(2,1)}), bf16[8,64,512]{2,1,0:T(8,128)(2,1)S(1)}, u32[]{:S(2)}, u32[]{:S(2)}) async-start(bf16[8,64,512]{2,1,0:T(8,128)(2,1)} %shard_map.127), calls=%async_computation.21 | async-start | bytes 1048576 | tf_op jit(solution)/shard_map/all_to_all | solution.py:33
  599.0 3.4 collective-permute-start.36
  (40 other events, 307.5 us)

commit v2 on v1

v2 whole, which is shorter than its diff:
```python
import functools
import math

import jax
import jax.numpy as jnp
from jax import lax
from jax.experimental import pallas as pl
from jax.experimental.pallas import tpu as pltpu
from jax.sharding import Mesh
from jax.sharding import PartitionSpec as P

HD = 128
SLOTS = 2
EPS = 1e-05
ROWS = 64


def swap(x):
    return lax.ppermute(x, "core", [(0, 1), (1, 0)])


def exchange(blocks):
    flat = blocks.reshape(blocks.shape[0] * blocks.shape[1], blocks.shape[2])
    moved = lax.all_to_all(flat, "chip", split_axis=0, concat_axis=0, tiled=True)
    return moved.reshape(blocks.shape)


def dot(a, b):
    return jnp.dot(a, b, preferred_element_type=jnp.float32)


def turn(values, cosine, sine):
    return values * cosine + pltpu.roll(values, HD // 2, 1) * sine


def table_kernel(parts, ctx_ref, cos_ref, sin_ref, fresh_ref, done_ref):
    chunks, rows, _ = cos_ref.shape
    lane = lax.broadcasted_iota(jnp.int32, (1, HD), 1)
    upper = lane >= HD // 2
    index = jnp.where(upper, lane - HD // 2, lane).astype(jnp.float32)
    freqs = jnp.exp(index * (-2.0 * math.log(500000.0) / HD))
    row = lax.broadcasted_iota(jnp.int32, (rows, HD), 0)
    for c in range(chunks):
        positions = ctx_ref[c // parts] + (c % parts) * rows + row
        angles = positions.astype(jnp.float32) * freqs
        cos_ref[c] = jnp.cos(angles)
        sine = jnp.sin(angles)
        sin_ref[c] = jnp.where(upper, sine, -sine)
    fresh_ref[...] = jnp.zeros_like(fresh_ref)
    done_ref[...] = jnp.zeros_like(done_ref)


def project_kernel(x_ref, gain_ref, mine_ref, other_ref, pair_ref, keep_ref, give_ref):
    n_chip, rows, width = x_ref.shape
    columns = mine_ref.shape[1]
    square = jnp.zeros((rows, 1), jnp.float32)
    parts = []
    core = lax.axis_index("core")
    for j in range(n_chip):
        part = x_ref[j].astype(jnp.float32)
        square += jnp.sum(part * part, axis=-1, keepdims=True)
        parts.append((part * gain_ref[:, strip(j, core, width)]).astype(jnp.bfloat16))
    scaled = jnp.concatenate(parts, axis=1)
    keep_ref[:, :columns] = dot(scaled, mine_ref[...])
    give_ref[:, :columns] = dot(scaled, other_ref[...])
    pair = dot(scaled, pair_ref[...])
    squares = jnp.broadcast_to(square, (rows, HD))
    for ref in (keep_ref, give_ref):
        ref[:, columns : columns + 2 * HD] = pair
        ref[:, columns + 2 * HD :] = squares


def attend_kernel(
    depth, step, ctx_ref, keep_ref, got_ref, cos_ref, sin_ref, held_ref, fresh_ref, attended_ref,
    new_ref,
):
    rows, columns = attended_ref.shape
    chunks, parts = cos_ref.shape[0], new_ref.shape[1] // rows
    index = step - lax.axis_index("section")
    valid = jnp.logical_and(index >= 0, index < chunks)
    index = jnp.clip(index, 0, chunks - 1)
    batch, offset = index // parts, (index % parts) * rows
    length = ctx_ref[batch]
    cached = held_ref.shape[1]
    span = fresh_ref.shape[1]
    total = keep_ref[...] + got_ref[...]
    square = total[:, columns + 2 * HD : columns + 2 * HD + 1]
    scale = lax.rsqrt(square / depth + EPS)
    cosine = cos_ref[index] * scale
    sine = sin_ref[index] * scale
    pair = total[:, columns : columns + 2 * HD]
    low = HD // 2
    keys = jnp.concatenate([pair[:, :low], pair[:, HD : HD + low]], axis=1)
    values = jnp.concatenate([pair[:, low:HD], pair[:, HD + low :]], axis=1) * scale
    new_ref[...] = fresh_ref[...]

    @pl.when(valid)
    def _():
        place = pl.ds(pl.multiple_of(offset, rows), rows)
        new_ref[batch, place, :HD] = turn(keys, cosine, sine).astype(jnp.bfloat16)
        new_ref[batch, place, HD:] = values.astype(jnp.bfloat16)

    live = lax.broadcasted_iota(jnp.int32, (1, cached), 1) < length
    row = lax.broadcasted_iota(jnp.int32, (rows, span), 0) + offset
    causal = lax.broadcasted_iota(jnp.int32, (rows, span), 1) <= row
    heads = columns // HD
    group = max(1, min(heads, 128 // rows))
    causal = jnp.concatenate([causal] * group, axis=0)
    root = 1.0 / math.sqrt(HD)
    contract = (((1,), (1,)), ((), ()))
    for base in range(0, heads, group):
        queries = jnp.concatenate(
            [
                turn(total[:, h * HD : (h + 1) * HD], cosine, sine).astype(jnp.bfloat16)
                for h in range(base, base + group)
            ],
            axis=0,
        )
        scores = lax.dot_general(
            queries, held_ref[batch, :, :HD], contract, preferred_element_type=jnp.float32
        )
        scores = jnp.where(live, scores, -1e30)
        recent = lax.dot_general(
            queries, new_ref[batch, :, :HD], contract, preferred_element_type=jnp.float32
        )
        recent = jnp.where(causal, recent, -1e30)
        top = jnp.maximum(
            jnp.max(scores, axis=-1, keepdims=True), jnp.max(recent, axis=-1, keepdims=True)
        )
        scores = jnp.exp((scores - top) * root)
        recent = jnp.exp((recent - top) * root)
        weight = jnp.sum(scores, axis=-1, keepdims=True) + jnp.sum(recent, axis=-1, keepdims=True)
        mixed = dot(scores.astype(jnp.bfloat16), held_ref[batch, :, HD:]) + dot(
            recent.astype(jnp.bfloat16), new_ref[batch, :, HD:]
        )
        mixed = (mixed / weight).astype(jnp.bfloat16)
        for h in range(group):
            attended_ref[:, (base + h) * HD : (base + h + 1) * HD] = mixed[
                h * rows : (h + 1) * rows
            ]


def out_kernel(mine_ref, got_ref, own_ref, other_ref, partial_ref):
    n_chip, _, width = partial_ref.shape
    for j in range(n_chip):
        columns = slice(j * width, (j + 1) * width)
        partial = dot(mine_ref[...], own_ref[:, columns]) + dot(got_ref[...], other_ref[:, columns])
        partial_ref[j] = partial.astype(jnp.bfloat16)


def enter_kernel(step, incoming_ref, inputs_ref, layer_ref, copies_ref):
    layer_ref[...] = incoming_ref[...]

    @pl.when(lax.axis_index("section") == 0)
    def _():
        layer_ref[...] = inputs_ref[step]

    for j in range(copies_ref.shape[0]):
        copies_ref[j] = layer_ref[...]


def settle_kernel(step, pieces_ref, layer_ref, done_ref, send_ref, new_ref):
    chunks = done_ref.shape[0]
    section = lax.axis_index("section")
    index = step - section
    total = layer_ref[...].astype(jnp.float32)
    summed = pieces_ref[0].astype(jnp.float32)
    for j in range(1, pieces_ref.shape[0]):
        summed += pieces_ref[j].astype(jnp.float32)
    updated = (total + summed).astype(jnp.bfloat16)
    send_ref[...] = updated
    new_ref[...] = done_ref[...]

    @pl.when(jnp.logical_and(index >= 0, index < chunks))
    def _():
        new_ref[jnp.clip(index, 0, chunks - 1)] = updated


def share_kernel(fresh_ref, copies_ref):
    micro, span, _ = fresh_ref.shape
    half = span // 2
    rows = pl.ds(pl.multiple_of(lax.axis_index("core") * half, half), half)
    for m in range(micro):
        block = fresh_ref[m, rows, :]
        for j in range(copies_ref.shape[0]):
            copies_ref[j, m * half : (m + 1) * half, :] = block


def pick_kernel(holders_ref, blocks_ref, mine_ref, other_ref):
    heads, micro = holders_ref.shape
    count = heads * micro
    half = mine_ref.shape[1]
    holders = [holders_ref[e // micro, e % micro] for e in range(count)]
    core = lax.axis_index("core")
    first = 2 * lax.axis_index("chip")
    for ref, member in ((mine_ref, first + core), (other_ref, first + 1 - core)):
        ref[...] = jnp.zeros_like(ref)
        slot = jnp.int32(0)
        for e in range(count):
            here = holders[e] == member

            @pl.when(here)
            def _(slot=slot, e=e, ref=ref):
                ref[slot] = blocks_ref[e // micro, (e % micro) * half : (e % micro + 1) * half, :]

            slot = jnp.minimum(slot + here.astype(jnp.int32), SLOTS - 1)


def move(copies, sems):
    started = [
        pltpu.make_async_copy(source, target, sems.at[i])
        for i, (source, target) in enumerate(copies)
    ]
    for copy in started:
        copy.start()
    for copy in started:
        copy.wait()


def strip(chip, core, width):
    return pl.ds(pl.multiple_of((2 * chip + core) * width, width), width)


def give_kernel(width, query_ref, pair_ref, give_query_ref, give_pair_ref, sems):
    other = 1 - lax.axis_index("core")
    copies = []
    for j in range(query_ref.shape[0] // (2 * width)):
        rows, here = strip(j, other, width), pl.ds(j * width, width)
        copies.append((query_ref.at[rows], give_query_ref.at[here]))
        copies.append((pair_ref.at[rows], give_pair_ref.at[here]))
    move(copies, sems)


def keep_kernel(width, query_ref, out_ref, own_query_ref, own_out_ref, give_out_ref, sems):
    core = lax.axis_index("core")
    copies = []
    for j in range(query_ref.shape[0] // (2 * width)):
        mine, here = strip(j, core, width), pl.ds(j * width, width)
        copies.append((query_ref.at[mine], own_query_ref.at[here]))
        copies.append((out_ref.at[:, mine], own_out_ref.at[:, here]))
        copies.append((out_ref.at[:, strip(j, 1 - core, width)], give_out_ref.at[:, here]))
    move(copies, sems)


def join_kernel(
    n_chip, pair_ref, got_pair_ref, cache_ref, got_cache_ref, got_query_ref,
    both_ref, context_ref, other_query_ref, sems,
):
    width = pair_ref.shape[0] // (2 * n_chip)
    core = lax.axis_index("core")
    length = cache_ref.shape[1]
    mine, theirs = pl.ds(pl.multiple_of(core * HD, HD), HD), pl.ds(pl.multiple_of((1 - core) * HD, HD), HD)
    early = pl.ds(pl.multiple_of(core * length, length), length)
    late = pl.ds(pl.multiple_of((1 - core) * length, length), length)
    copies = [
        (got_pair_ref, both_ref.at[:, theirs]),
        (cache_ref, context_ref.at[:, early]),
        (got_cache_ref, context_ref.at[:, late]),
        (got_query_ref, other_query_ref),
    ]
    for j in range(n_chip):
        copies.append(
            (pair_ref.at[strip(j, core, width)], both_ref.at[pl.ds(j * width, width), mine])
        )
    move(copies, sems)


def load_kernel(source_ref, target_ref, sems):
    move([(source_ref, target_ref)], sems)


def shuffle(kernel, out, inputs, copies):
    return pl.pallas_call(
        kernel,
        out_shape=out,
        in_specs=[pl.BlockSpec(memory_space=pl.ANY)] * inputs,
        out_specs=jax.tree.map(lambda _: pl.BlockSpec(memory_space=pl.ANY), out),
        scratch_shapes=[pltpu.SemaphoreType.DMA((copies,))],
        compiler_params=pltpu.CompilerParams(vmem_limit_bytes=2**20),
    )


def fast(x):
    return pltpu.with_memory_space_constraint(x, pltpu.VMEM)


def slow(x):
    return pltpu.with_memory_space_constraint(x, pltpu.HBM)


def call(kernel, out, flops, scalars, arrays, limit):
    return pl.pallas_call(
        kernel,
        out_shape=out,
        in_specs=[pl.BlockSpec(memory_space=pltpu.SMEM)] * scalars
        + [pl.BlockSpec(memory_space=pltpu.VMEM)] * arrays,
        out_specs=jax.tree.map(lambda _: pl.BlockSpec(memory_space=pltpu.VMEM), out),
        compiler_params=pltpu.CompilerParams(vmem_limit_bytes=limit * 2**20),
        cost_estimate=pl.CostEstimate(flops=flops, bytes_accessed=2**20, transcendentals=0),
    )


def shards(hidden_in, norm_gain, w_query, w_key_value, w_out, cache, ctx_len, placement):
    n_section = lax.axis_size("section")
    n_chip = lax.axis_size("chip")
    micro, span, width = hidden_in.shape
    rows = min(ROWS, span)
    parts = span // rows
    chunks = micro * parts
    steps = n_section + chunks - 1
    depth = n_chip * 2 * width
    side = depth // 2
    columns = w_query.shape[2]
    bf16, f32 = jnp.bfloat16, jnp.float32
    shape = jax.ShapeDtypeStruct

    def vmem(*dims):
        return pltpu.VMEM(dims, bf16)

    wq, wkv, wo, held = (slow(x[0]) for x in (w_query, w_key_value, w_out, cache))
    inputs = fast(hidden_in.reshape(chunks, rows, width))
    gain = fast(norm_gain)
    angle = shape((chunks, rows, HD), f32)
    state = shape((micro, span, 2 * HD), bf16)
    done_shape = shape((chunks, rows, width), bf16)
    cosines, sines, fresh, done = call(
        functools.partial(table_kernel, parts), (angle, angle, state, done_shape), 2**20, 1, 0, 4
    )(ctx_len)

    give_query, give_pair = shuffle(
        functools.partial(give_kernel, width), (vmem(side, columns), vmem(side, HD)), 2, 2 * n_chip
    )(wq, wkv)
    got_query, got_pair, got_cache = swap(give_query), swap(give_pair), swap(cache[0])
    layer_in, cosines, sines, fresh, done, _ = lax.optimization_barrier(
        (hidden_in[0, :rows], cosines, sines, fresh, done, give_query)
    )
    features = exchange(jnp.broadcast_to(layer_in[None], (n_chip, rows, width)))
    features, w_query, w_out = lax.optimization_barrier((features, w_query, w_out))
    wq, wo = slow(w_query[0]), slow(w_out[0])
    wq_own, wo_own, give_out = shuffle(
        functools.partial(keep_kernel, width),
        (vmem(side, columns), vmem(columns, side), vmem(columns, side)),
        2,
        3 * n_chip,
    )(wq, wo)
    got_out = swap(give_out)
    w_pair, context, wq_other = shuffle(
        functools.partial(join_kernel, n_chip),
        (vmem(side, 2 * HD), vmem(micro, 2 * cache.shape[2], 2 * HD), vmem(side, columns)),
        5,
        4 + n_chip,
    )(wkv, slow(got_pair), held, slow(got_cache), slow(got_query))
    wo_other = None
    wq_own, wo_own, w_pair, context, wq_other = (
        fast(v) for v in (wq_own, wo_own, w_pair, context, wq_other)
    )

    packed = shape((rows, columns + 3 * HD), f32)
    block = shape((rows, columns), bf16)
    project = call(
        project_kernel, (packed, packed), rows * depth * 2 * (columns + HD), 0, 5, 4
    )
    finish = call(
        out_kernel, shape((n_chip, rows, width), bf16), 2 * rows * columns * depth, 0, 4, 4
    )
    for step in range(steps):
        if step > 0:
            if step < chunks:
                layer_in, copies = call(
                    functools.partial(enter_kernel, step),
                    (block, shape((n_chip, rows, width), bf16)),
                    2**20,
                    0,
                    2,
                    4,
                )(layer_in, inputs)
            else:
                copies = jnp.broadcast_to(layer_in[None], (n_chip, rows, width))
            features = exchange(copies)
        keep, give = project(features, gain, wq_own, wq_other, w_pair)
        attend = call(
            functools.partial(attend_kernel, depth, step),
            (block, state),
            4 * rows * columns * (context.shape[1] + span),
            1,
            6,
            12,
        )
        attended, fresh = attend(ctx_len, keep, swap(give), cosines, sines, context, fresh)
        if step == 0:
            wo_other = fast(shuffle(load_kernel, vmem(columns, side), 1, 1)(slow(got_out)))
        partial = finish(attended, swap(attended), wo_own, wo_other)
        if step + 1 == steps:
            partial, fresh = lax.optimization_barrier((partial, fresh))
            copies = call(
                share_kernel, shape((n_chip, micro * span // 2, 2 * HD), bf16), 2**20, 0, 1, 4
            )(fresh)
            blocks = exchange(copies)
        pieces = exchange(partial)
        settle = call(
            functools.partial(settle_kernel, step), (block, done_shape), 2**20, 0, 3, 4
        )
        send, done = settle(pieces, layer_in, done)
        if step + 1 < steps:
            route = [
                (i, i + 1)
                for i in range(max(0, step - chunks + 1), min(step, n_section - 2) + 1)
            ]
            layer_in = lax.ppermute(send, "section", route)
    outputs = done.reshape(micro, span, width)

    slots = shape((SLOTS, span // 2, 2 * HD), bf16)
    mine, other = call(pick_kernel, (slots, slots), 2**20, 1, 1, 4)(placement[0], blocks)
    other = swap(other)
    store = jnp.where(
        lax.axis_index("core") == 0,
        jnp.concatenate([mine, other], axis=1),
        jnp.concatenate([other, mine], axis=1),
    )
    return (outputs[None], store[None])


def solution(mesh):
    n_section, n_tp = mesh.devices.shape
    fine = Mesh(mesh.devices.reshape(n_section, n_tp // 2, 2), ("section", "chip", "core"))
    tp = ("chip", "core")
    in_specs = (
        P(None, None, tp),
        P("section", None),
        P("section", None, tp),
        P("section", None, tp),
        P("section", tp, None),
        P("section", None, tp, None),
        P(),
        P("section", None, None),
    )
    out_specs = (P("section", None, None, tp), P("section", tp, None, None))
    return jax.shard_map(shards, mesh=fine, in_specs=in_specs, out_specs=out_specs, check_vma=False)
```

time: 613 us -> 489 us (0.80)
  the two profiles are of different devices: /device:TPU:73 before, /device:TPU:70 now
where the time goes in v2:
time: 489 us; the launch traced here: 479 us
  blocking collectives  261 us (53%)
  waiting for transfers between devices  105 us (21%)
  Pallas kernels  80.5 us (16%)
  starting transfers between devices  22.6 us (5%)
  local copies, waits for them, and re-layouts  7.75 us (2%)
    all_to_all x21, blocking collectives, exchange(): lax.all_to_all(flat, 'chip', split_axis=0, concat_axis=0, tiled=True)  261 us
    ppermute x10, waiting for transfers between devices, shards(): layer_in = lax.ppermute(send, 'section', route)  51.4 us
    ppermute x27, waiting for transfers between devices, swap(): return lax.ppermute(x, 'core', [(0, 1), (1, 0)])  36.8 us
    pallas_call x11, Pallas kernels, shards(): attend(ctx_len, keep, swap(give), cosines, sines, context, fresh)  23.8 us
    pallas_call x11, Pallas kernels, shards(): keep, give = project(features, gain, wq_own, wq_other, w_pair)  21.9 us
    pallas_call x11, Pallas kernels, shards(): partial = finish(attended, swap(attended), wo_own, wo_other)  18 us
    all_to_all x2, waiting for transfers between devices, exchange(): lax.all_to_all(flat, 'chip', split_axis=0, concat_axis=0, tiled=True)  17 us
  transfers between devices with their start and end apart: 39, of which 29 were waited for; matrix products, arithmetic and copies ran while one was open for 0% of the time, Pallas kernels for 3%

profile of v2, /device:TPU:70, one launch (start us, length us, event | category | flops | bytes accessed | tf_op | source)
XLA Modules:
  0.0 479.3 jit_solution(16437596427963409055)
XLA Ops:
  8.6 5.5 %all-to-all-start = ((bf16[8,64,512]{2,1,0:T(8,128)(2,1)}), bf16[8,64,512]{2,1,0:T(8,128)(2,1)S(1)}, u32[]{:S(2)}, u32[]{:S(2)}) async-start(bf16[8,64,512]{2,1,0:T(8,128)(2,1)} %broadcast_in_dim.16), calls=%async_computation | async-start | bytes 1048576 | tf_op jit(solution)/shard_map/all_to_all | solution.py:24
  14.2 9.5 %all-to-all-done.x_ref = bf16[8,64,512]{2,1,0:T(8,128)(2,1)S(1)} async-done(((bf16[8,64,512]{2,1,0:T(8,128)(2,1)}), bf16[8,64,512]{2,1,0:T(8,128)(2,1)S(1)}, u32[]{:S(2)}, u32[]{:S(2)}) %all-to-all-start) | async-done | bytes 524320 | tf_op jit(solution)/shard_map/all_to_all | solution.py:24
  23.7 4.9 %shard_map.97 = (bf16[4096,512]{1,0:T(8,128)(2,1)S(1)}, bf16[512,4096]{1,0:T(8,128)(2,1)S(1)}, bf16[512,4096]{1,0:T(8,128)(2,1)S(1)}) custom-call(bf16[8192,512]{1,0:T(8,128)(2,1)} %bitcast.17, bf16[512,8192]{1,0:T(8,128)(2,1)} %bitcast.18), custom_call_target="tpu_custom_call" | custom-call | tf_op jit(solution)/shard_map/pallas_call | solution.py:340
  29.3 8.0 %collective-permute-done.1.got_cache_ref = bf16[2,1024,256]{2,1,0:T(8,128)(2,1)S(1)} collective-permute-done((bf16[2,1024,256]{2,1,0:T(8,128)(2,1)S(1)}, bf16[2,1024,256]{2,1,0:T(8,128)(2,1)S(1)}, u32[]{:S(2)}, u32[]{:S(2)}) %collective-permute-start.1) | collective-permute-done | bytes 1048608 | tf_op jit(solution)/shard_map/ppermute | solution.py:19
  39.8 3.4 shard_map.98
  55.0 13.4 %all_to_all.138.pieces_ref = bf16[8,64,512]{2,1,0:T(8,128)(2,1)S(1)} all-to-all(bf16[8,64,512]{2,1,0:T(8,128)(2,1)S(1)} %shard_map.102), channel_id=1, replica_groups=mesh['section'=8,'chip'=8,'core'=2] {'chip'}, dimensions={0} | all-to-all | bytes 1048576 | tf_op jit(solution)/shard_map/all_to_all | solution.py:24
  69.3 12.0 %all_to_all.139.x_ref = bf16[8,64,512]{2,1,0:T(8,128)(2,1)S(1)} all-to-all(bf16[8,64,512]{2,1,0:T(8,128)(2,1)S(1)} %get-tuple-element.121), channel_id=1, replica_groups=mesh['section'=8,'chip'=8,'core'=2] {'chip'}, dimensions={0} | all-to-all | bytes 1048576 | tf_op jit(solution)/shard_map/all_to_all | solution.py:24
  89.9 12.9 %all_to_all.140.pieces_ref = bf16[8,64,512]{2,1,0:T(8,128)(2,1)S(1)} all-to-all(bf16[8,64,512]{2,1,0:T(8,128)(2,1)S(1)} %shard_map.107), channel_id=1, replica_groups=mesh['section'=8,'chip'=8,'core'=2] {'chip'}, dimensions={0} | all-to-all | bytes 1048576 | tf_op jit(solution)/shard_map/all_to_all | solution.py:24
  103.7 12.1 %all_to_all.141.x_ref = bf16[8,64,512]{2,1,0:T(8,128)(2,1)S(1)} all-to-all(bf16[8,64,512]{2,1,0:T(8,128)(2,1)S(1)} %get-tuple-element.129), channel_id=1, replica_groups=mesh['section'=8,'chip'=8,'core'=2] {'chip'}, dimensions={0} | all-to-all | bytes 1048576 | tf_op jit(solution)/shard_map/all_to_all | solution.py:24
  124.3 12.9 %all_to_all.142.pieces_ref = bf16[8,64,512]{2,1,0:T(8,128)(2,1)S(1)} all-to-all(bf16[8,64,512]{2,1,0:T(8,128)(2,1)S(1)} %shard_map.112), channel_id=1, replica_groups=mesh['section'=8,'chip'=8,'core'=2] {'chip'}, dimensions={0} | all-to-all | bytes 1048576 | tf_op jit(solution)/shard_map/all_to_all | solution.py:24
  138.1 12.1 %all_to_all.143.x_ref = bf16[8,64,512]{2,1,0:T(8,128)(2,1)S(1)} all-to-all(bf16[8,64,512]{2,1,0:T(8,128)(2,1)S(1)} %get-tuple-element.137), channel_id=1, replica_groups=mesh['section'=8,'chip'=8,'core'=2] {'chip'}, dimensions={0} | all-to-all | bytes 1048576 | tf_op jit(solution)/shard_map/all_to_all | solution.py:24
  158.8 12.9 %all_to_all.144.pieces_ref = bf16[8,64,512]{2,1,0:T(8,128)(2,1)S(1)} all-to-all(bf16[8,64,512]{2,1,0:T(8,128)(2,1)S(1)} %shard_map.117), channel_id=1, replica_groups=mesh['section'=8,'chip'=8,'core'=2] {'chip'}, dimensions={0} | all-to-all | bytes 1048576 | tf_op jit(solution)/shard_map/all_to_all | solution.py:24
  172.5 12.1 %all_to_all.145.x_ref = bf16[8,64,512]{2,1,0:T(8,128)(2,1)S(1)} all-to-all(bf16[8,64,512]{2,1,0:T(8,128)(2,1)S(1)} %broadcast_in_dim.17), channel_id=1, replica_groups=mesh['section'=8,'chip'=8,'core'=2] {'chip'}, dimensions={0} | all-to-all | bytes 1048576 | tf_op jit(solution)/shard_map/all_to_all | solution.py:24
  193.4 12.9 %all_to_all.146.pieces_ref = bf16[8,64,512]{2,1,0:T(8,128)(2,1)S(1)} all-to-all(bf16[8,64,512]{2,1,0:T(8,128)(2,1)S(1)} %shard_map.121), channel_id=1, replica_groups=mesh['section'=8,'chip'=8,'core'=2] {'chip'}, dimensions={0} | all-to-all | bytes 1048576 | tf_op jit(solution)/shard_map/all_to_all | solution.py:24
  207.1 12.1 %all_to_all.147.x_ref = bf16[8,64,512]{2,1,0:T(8,128)(2,1)S(1)} all-to-all(bf16[8,64,512]{2,1,0:T(8,128)(2,1)S(1)} %broadcast_in_dim.18), channel_id=1, replica_groups=mesh['section'=8,'chip'=8,'core'=2] {'chip'}, dimensions={0} | all-to-all | bytes 1048576 | tf_op jit(solution)/shard_map/all_to_all | solution.py:24
  227.8 12.9 %all_to_all.148.pieces_ref = bf16[8,64,512]{2,1,0:T(8,128)(2,1)S(1)} all-to-all(bf16[8,64,512]{2,1,0:T(8,128)(2,1)S(1)} %shard_map.125), channel_id=1, replica_groups=mesh['section'=8,'chip'=8,'core'=2] {'chip'}, dimensions={0} | all-to-all | bytes 1048576 | tf_op jit(solution)/shard_map/all_to_all | solution.py:24
  241.6 12.1 %all_to_all.149.x_ref = bf16[8,64,512]{2,1,0:T(8,128)(2,1)S(1)} all-to-all(bf16[8,64,512]{2,1,0:T(8,128)(2,1)S(1)} %broadcast_in_dim.19), channel_id=1, replica_groups=mesh['section'=8,'chip'=8,'core'=2] {'chip'}, dimensions={0} | all-to-all | bytes 1048576 | tf_op jit(solution)/shard_map/all_to_all | solution.py:24
  262.5 12.9 %all_to_all.150.pieces_ref = bf16[8,64,512]{2,1,0:T(8,128)(2,1)S(1)} all-to-all(bf16[8,64,512]{2,1,0:T(8,128)(2,1)S(1)} %shard_map.129), channel_id=1, replica_groups=mesh['section'=8,'chip'=8,'core'=2] {'chip'}, dimensions={0} | all-to-all | bytes 1048576 | tf_op jit(solution)/shard_map/all_to_all | solution.py:24
  276.8 27.2 %collective-permute-done.24.layer_ref = bf16[64,512]{1,0:T(8,128)(2,1)S(1)} collective-permute-done((bf16[64,512]{1,0:T(8,128)(2,1)S(1)}, bf16[64,512]{1,0:T(8,128)(2,1)S(1)}, u32[]{:S(2)}, u32[]{:S(2)}) %collective-permute-start.24) | collective-permute-done | bytes 65568 | tf_op jit(solution)/shard_map/ppermute | solution.py:409
  304.0 11.5 %all_to_all.151.x_ref = bf16[8,64,512]{2,1,0:T(8,128)(2,1)S(1)} all-to-all(bf16[8,64,512]{2,1,0:T(8,128)(2,1)S(1)} %broadcast_in_dim.20), channel_id=1, replica_groups=mesh['section'=8,'chip'=8,'core'=2] {'chip'}, dimensions={0} | all-to-all | bytes 1048576 | tf_op jit(solution)/shard_map/all_to_all | solution.py:24
  324.2 12.7 %all_to_all.152.pieces_ref = bf16[8,64,512]{2,1,0:T(8,128)(2,1)S(1)} all-to-all(bf16[8,64,512]{2,1,0:T(8,128)(2,1)S(1)} %shard_map.133), channel_id=1, replica_groups=mesh['section'=8,'chip'=8,'core'=2] {'chip'}, dimensions={0} | all-to-all | bytes 1048576 | tf_op jit(solution)/shard_map/all_to_all | solution.py:24
  338.3 9.3 %collective-permute-done.27.layer_ref = bf16[64,512]{1,0:T(8,128)(2,1)S(1)} collective-permute-done((bf16[64,512]{1,0:T(8,128)(2,1)S(1)}, bf16[64,512]{1,0:T(8,128)(2,1)S(1)}, u32[]{:S(2)}, u32[]{:S(2)}) %collective-permute-start.27) | collective-permute-done | bytes 65568 | tf_op jit(solution)/shard_map/ppermute | solution.py:409
  347.6 11.5 %all_to_all.153.x_ref = bf16[8,64,512]{2,1,0:T(8,128)(2,1)S(1)} all-to-all(bf16[8,64,512]{2,1,0:T(8,128)(2,1)S(1)} %broadcast_in_dim.21), channel_id=1, replica_groups=mesh['section'=8,'chip'=8,'core'=2] {'chip'}, dimensions={0} | all-to-all | bytes 1048576 | tf_op jit(solution)/shard_map/all_to_all | solution.py:24
  367.8 12.7 %all_to_all.154.pieces_ref = bf16[8,64,512]{2,1,0:T(8,128)(2,1)S(1)} all-to-all(bf16[8,64,512]{2,1,0:T(8,128)(2,1)S(1)} %shard_map.137), channel_id=1, replica_groups=mesh['section'=8,'chip'=8,'core'=2] {'chip'}, dimensions={0} | all-to-all | bytes 1048576 | tf_op jit(solution)/shard_map/all_to_all | solution.py:24
  381.9 8.4 %collective-permute-done.30.layer_ref = bf16[64,512]{1,0:T(8,128)(2,1)S(1)} collective-permute-done((bf16[64,512]{1,0:T(8,128)(2,1)S(1)}, bf16[64,512]{1,0:T(8,128)(2,1)S(1)}, u32[]{:S(2)}, u32[]{:S(2)}) %collective-permute-start.30) | collective-permute-done | bytes 65568 | tf_op jit(solution)/shard_map/ppermute | solution.py:409
  390.4 11.7 %all_to_all.155.x_ref = bf16[8,64,512]{2,1,0:T(8,128)(2,1)S(1)} all-to-all(bf16[8,64,512]{2,1,0:T(8,128)(2,1)S(1)} %broadcast_in_dim.22), channel_id=1, replica_groups=mesh['section'=8,'chip'=8,'core'=2] {'chip'}, dimensions={0} | all-to-all | bytes 1048576 | tf_op jit(solution)/shard_map/all_to_all | solution.py:24
  410.8 12.7 %all_to_all.156.pieces_ref = bf16[8,64,512]{2,1,0:T(8,128)(2,1)S(1)} all-to-all(bf16[8,64,512]{2,1,0:T(8,128)(2,1)S(1)} %shard_map.141), channel_id=1, replica_groups=mesh['section'=8,'chip'=8,'core'=2] {'chip'}, dimensions={0} | all-to-all | bytes 1048576 | tf_op jit(solution)/shard_map/all_to_all | solution.py:24
  424.9 6.5 %collective-permute-done.33.layer_ref = bf16[64,512]{1,0:T(8,128)(2,1)S(1)} collective-permute-done((bf16[64,512]{1,0:T(8,128)(2,1)S(1)}, bf16[64,512]{1,0:T(8,128)(2,1)S(1)}, u32[]{:S(2)}, u32[]{:S(2)}) %collective-permute-start.33) | collective-permute-done | bytes 65568 | tf_op jit(solution)/shard_map/ppermute | solution.py:409
  431.5 11.5 %all_to_all.157.x_ref = bf16[8,64,512]{2,1,0:T(8,128)(2,1)S(1)} all-to-all(bf16[8,64,512]{2,1,0:T(8,128)(2,1)S(1)} %broadcast_in_dim.23), channel_id=1, replica_groups=mesh['section'=8,'chip'=8,'core'=2] {'chip'}, dimensions={0} | all-to-all | bytes 1048576 | tf_op jit(solution)/shard_map/all_to_all | solution.py:24
  452.5 12.7 %all_to_all.158.blocks_ref = bf16[8,128,256]{2,1,0:T(8,128)(2,1)S(1)} all-to-all(bf16[8,128,256]{2,1,0:T(8,128)(2,1)S(1)} %shard_map.147), channel_id=1, replica_groups=mesh['section'=8,'chip'=8,'core'=2] {'chip'}, dimensions={0} | all-to-all | bytes 1048576 | tf_op jit(solution)/shard_map/all_to_all | solution.py:24
  465.2 3.5 all-to-all-start.21
  469.8 7.6 %all-to-all-done.21.pieces_ref = bf16[8,64,512]{2,1,0:T(8,128)(2,1)S(1)} async-done(((bf16[8,64,512]{2,1,0:T(8,128)(2,1)}), bf16[8,64,512]{2,1,0:T(8,128)(2,1)S(1)}, u32[]{:S(2)}, u32[]{:S(2)}) %all-to-all-start.21) | async-done | bytes 524320 | tf_op jit(solution)/shard_map/all_to_all | solution.py:24
  (152 shorter events, 123.0 us)
Async XLA Ops:
  8.6 15.0 %all-to-all-start = ((bf16[8,64,512]{2,1,0:T(8,128)(2,1)}), bf16[8,64,512]{2,1,0:T(8,128)(2,1)S(1)}, u32[]{:S(2)}, u32[]{:S(2)}) async-start(bf16[8,64,512]{2,1,0:T(8,128)(2,1)} %broadcast_in_dim.16), calls=%async_computation | async-start | bytes 1048576 | tf_op jit(solution)/shard_map/all_to_all | solution.py:24
  14.2 24.7 %collective-permute-start.2 = (bf16[4096,512]{1,0:T(8,128)(2,1)}, bf16[4096,512]{1,0:T(8,128)(2,1)}, u32[]{:S(2)}, u32[]{:S(2)}) collective-permute-start(bf16[4096,512]{1,0:T(8,128)(2,1)} %copy-done.4), channel_id=1, source_target_pairs={{0,1},{1,0},{2,3},{3,2},{4,5},{5,4},{6,7},{7,6},{8,9},{9,8},{10,11... | collective-permute-start | bytes 12582920 | tf_op jit(solution)/shard_map/ppermute | solution.py:19
  28.6 20.6 %collective-permute-start.5 = (bf16[512,4096]{1,0:T(8,128)(2,1)S(1)}, bf16[512,4096]{1,0:T(8,128)(2,1)S(1)}, u32[]{:S(2)}, u32[]{:S(2)}) collective-permute-start(bf16[512,4096]{1,0:T(8,128)(2,1)S(1)} %get-tuple-element.118), channel_id=1, source_target_pairs={{0,1},{1,0},{2,3},{3,2},{4,5},{5,4},{6,7},{7,6},{8,9},{9,8},{10,11... | collective-permute-start | bytes 12582920 | tf_op jit(solution)/shard_map/ppermute | solution.py:19
  28.7 8.6 %collective-permute-start.1 = (bf16[2,1024,256]{2,1,0:T(8,128)(2,1)S(1)}, bf16[2,1024,256]{2,1,0:T(8,128)(2,1)S(1)}, u32[]{:S(2)}, u32[]{:S(2)}) collective-permute-start(bf16[2,1024,256]{2,1,0:T(8,128)(2,1)S(1)} %bitcast.22), channel_id=1, source_target_pairs={{0,1},{1,0},{2,3},{3,2},{4,5},{5,4},{6,7},{7,6},{8,9},{9,8},{10,11... | collective-permute-start | bytes 3145736 | tf_op jit(solution)/shard_map/ppermute | solution.py:19
  29.2 9.6 %collective-permute-start = (bf16[4096,128]{1,0:T(8,128)(2,1)S(1)}, bf16[4096,128]{1,0:T(8,128)(2,1)S(1)}, u32[]{:S(2)}, u32[]{:S(2)}) collective-permute-start(bf16[4096,128]{1,0:T(8,128)(2,1)S(1)} %get-tuple-element.107), channel_id=1, source_target_pairs={{0,1},{1,0},{2,3},{3,2},{4,5},{5,4},{6,7},{7,6},{8,9},{9,8},{10,11... | collective-permute-start | bytes 3145736 | tf_op jit(solution)/shard_map/ppermute | solution.py:19
  45.3 1.6 collective-permute-start.3
  48.9 4.5 collective-permute-start.4
  83.3 1.6 collective-permute-start.7
  87.0 1.3 collective-permute-start.8
  117.8 1.6 collective-permute-start.10
  121.4 1.3 collective-permute-start.11
  152.2 1.6 collective-permute-start.13
  155.9 1.3 collective-permute-start.14
  186.6 1.6 collective-permute-start.16
  190.5 1.3 collective-permute-start.17
  221.2 1.6 collective-permute-start.19
  255.7 1.6 collective-permute-start.22
  259.3 1.5 collective-permute-start.23
  275.5 28.5 %collective-permute-start.24 = (bf16[64,512]{1,0:T(8,128)(2,1)S(1)}, bf16[64,512]{1,0:T(8,128)(2,1)S(1)}, u32[]{:S(2)}, u32[]{:S(2)}) collective-permute-start(bf16[64,512]{1,0:T(8,128)(2,1)S(1)} %get-tuple-element.162), channel_id=1, source_target_pairs={{48,64},{64,80},{80,96},{96,112},{49,65},{65,81},{81,97},{97,113},... | collective-permute-start | bytes 196616 | tf_op jit(solution)/shard_map/ppermute | solution.py:409
  317.5 1.6 collective-permute-start.25
  321.3 1.3 collective-permute-start.26
  337.0 10.6 %collective-permute-start.27 = (bf16[64,512]{1,0:T(8,128)(2,1)S(1)}, bf16[64,512]{1,0:T(8,128)(2,1)S(1)}, u32[]{:S(2)}, u32[]{:S(2)}) collective-permute-start(bf16[64,512]{1,0:T(8,128)(2,1)S(1)} %get-tuple-element.168), channel_id=1, source_target_pairs={{64,80},{80,96},{96,112},{65,81},{81,97},{97,113},{66,82},{82,98},... | collective-permute-start | bytes 196616 | tf_op jit(solution)/shard_map/ppermute | solution.py:409
  361.1 1.6 collective-permute-start.28
  364.9 1.3 collective-permute-start.29
  380.6 9.7 %collective-permute-start.30 = (bf16[64,512]{1,0:T(8,128)(2,1)S(1)}, bf16[64,512]{1,0:T(8,128)(2,1)S(1)}, u32[]{:S(2)}, u32[]{:S(2)}) collective-permute-start(bf16[64,512]{1,0:T(8,128)(2,1)S(1)} %get-tuple-element.174), channel_id=1, source_target_pairs={{80,96},{96,112},{81,97},{97,113},{82,98},{98,114},{83,99},{99,115... | collective-permute-start | bytes 196616 | tf_op jit(solution)/shard_map/ppermute | solution.py:409
  404.1 1.6 collective-permute-start.31
  407.9 1.3 collective-permute-start.32
  423.6 7.8 %collective-permute-start.33 = (bf16[64,512]{1,0:T(8,128)(2,1)S(1)}, bf16[64,512]{1,0:T(8,128)(2,1)S(1)}, u32[]{:S(2)}, u32[]{:S(2)}) collective-permute-start(bf16[64,512]{1,0:T(8,128)(2,1)S(1)} %get-tuple-element.180), channel_id=1, source_target_pairs={{96,112},{97,113},{98,114},{99,115},{100,116},{101,117},{102,118},... | collective-permute-start | bytes 196616 | tf_op jit(solution)/shard_map/ppermute | solution.py:409
  445.0 1.6 collective-permute-start.34
  448.7 1.3 collective-permute-start.35
  465.2 12.1 %all-to-all-start.21 = ((bf16[8,64,512]{2,1,0:T(8,128)(2,1)}), bf16[8,64,512]{2,1,0:T(8,128)(2,1)S(1)}, u32[]{:S(2)}, u32[]{:S(2)}) async-start(bf16[8,64,512]{2,1,0:T(8,128)(2,1)} %shard_map.145), calls=%async_computation.21 | async-start | bytes 1048576 | tf_op jit(solution)/shard_map/all_to_all | solution.py:24
  469.7 8.5 %collective-permute-start.36 = (bf16[2,64,256]{2,1,0:T(8,128)(2,1)S(1)}, bf16[2,64,256]{2,1,0:T(8,128)(2,1)S(1)}, u32[]{:S(2)}, u32[]{:S(2)}) collective-permute-start(bf16[2,64,256]{2,1,0:T(8,128)(2,1)S(1)} %get-tuple-element.191), channel_id=1, source_target_pairs={{0,1},{1,0},{2,3},{3,2},{4,5},{5,4},{6,7},{7,6},{8,9},{9,8},{10,11... | collective-permute-start | bytes 196616 | tf_op jit(solution)/shard_map/ppermute | solution.py:19
  (17 other events, 71.1 us)

commit v3 on v2

--- a/solution.py
+++ b/solution.py
@@ -33,7 +33,9 @@
     return values * cosine + pltpu.roll(values, HD // 2, 1) * sine
 
 
-def table_kernel(parts, ctx_ref, cos_ref, sin_ref, fresh_ref, done_ref):
+def table_kernel(
+    parts, ctx_ref, inputs_ref, cos_ref, sin_ref, fresh_ref, done_ref, layer_ref, copies_ref
+):
     chunks, rows, _ = cos_ref.shape
     lane = lax.broadcasted_iota(jnp.int32, (1, HD), 1)
     upper = lane >= HD // 2
@@ -48,30 +50,34 @@
         sin_ref[c] = jnp.where(upper, sine, -sine)
     fresh_ref[...] = jnp.zeros_like(fresh_ref)
     done_ref[...] = jnp.zeros_like(done_ref)
-
-
-def project_kernel(x_ref, gain_ref, mine_ref, other_ref, pair_ref, keep_ref, give_ref):
+    layer_ref[...] = inputs_ref[0]
+    for j in range(copies_ref.shape[0]):
+        copies_ref[j] = inputs_ref[0]
+
+
+def project_kernel(x_ref, gain_ref, other_ref, pair_ref, scaled_ref, give_ref):
     n_chip, rows, width = x_ref.shape
-    columns = mine_ref.shape[1]
+    columns = other_ref.shape[1]
+    core = lax.axis_index("core")
     square = jnp.zeros((rows, 1), jnp.float32)
-    parts = []
-    core = lax.axis_index("core")
     for j in range(n_chip):
         part = x_ref[j].astype(jnp.float32)
         square += jnp.sum(part * part, axis=-1, keepdims=True)
-        parts.append((part * gain_ref[:, strip(j, core, width)]).astype(jnp.bfloat16))
-    scaled = jnp.concatenate(parts, axis=1)
-    keep_ref[:, :columns] = dot(scaled, mine_ref[...])
+        scaled_ref[:, j * width : (j + 1) * width] = (
+            part * gain_ref[:, strip(j, core, width)]
+        ).astype(jnp.bfloat16)
+    scaled = scaled_ref[...]
     give_ref[:, :columns] = dot(scaled, other_ref[...])
-    pair = dot(scaled, pair_ref[...])
-    squares = jnp.broadcast_to(square, (rows, HD))
-    for ref in (keep_ref, give_ref):
-        ref[:, columns : columns + 2 * HD] = pair
-        ref[:, columns + 2 * HD :] = squares
+    give_ref[:, columns : columns + 2 * HD] = dot(scaled, pair_ref[...])
+    give_ref[:, columns + 2 * HD :] = jnp.broadcast_to(square, (rows, HD))
+
+
+def query_kernel(scaled_ref, own_ref, keep_ref):
+    keep_ref[...] = dot(scaled_ref[...], own_ref[...])
 
 
 def attend_kernel(
-    depth, step, ctx_ref, keep_ref, got_ref, cos_ref, sin_ref, held_ref, fresh_ref, attended_ref,
+    depth, step, ctx_ref, keep_ref, give_ref, got_ref, cos_ref, sin_ref, held_ref, fresh_ref, attended_ref,
     new_ref,
 ):
     rows, columns = attended_ref.shape
@@ -83,12 +89,13 @@
     length = ctx_ref[batch]
     cached = held_ref.shape[1]
     span = fresh_ref.shape[1]
-    total = keep_ref[...] + got_ref[...]
-    square = total[:, columns + 2 * HD : columns + 2 * HD + 1]
+    total = keep_ref[...] + got_ref[:, :columns]
+    rest = give_ref[:, columns:] + got_ref[:, columns:]
+    square = rest[:, 2 * HD : 2 * HD + 1]
     scale = lax.rsqrt(square / depth + EPS)
     cosine = cos_ref[index] * scale
     sine = sin_ref[index] * scale
-    pair = total[:, columns : columns + 2 * HD]
+    pair = rest[:, : 2 * HD]
     low = HD // 2
     keys = jnp.concatenate([pair[:, :low], pair[:, HD : HD + low]], axis=1)
     values = jnp.concatenate([pair[:, low:HD], pair[:, HD + low :]], axis=1) * scale
@@ -140,12 +147,29 @@
             ]
 
 
-def out_kernel(mine_ref, got_ref, own_ref, other_ref, partial_ref):
-    n_chip, _, width = partial_ref.shape
+def out_kernel(mine_ref, own_ref, part_ref):
+    width = part_ref.shape[2]
+    for j in range(part_ref.shape[0]):
+        part_ref[j] = dot(mine_ref[...], own_ref[:, j * width : (j + 1) * width])
+
+
+def finish_kernel(part_ref, got_ref, other_ref, partial_ref):
+    width = part_ref.shape[2]
+    for j in range(part_ref.shape[0]):
+        more = dot(got_ref[...], other_ref[:, j * width : (j + 1) * width])
+        partial_ref[j] = (part_ref[j] + more).astype(jnp.bfloat16)
+
+
+def last_kernel(part_ref, got_ref, other_ref, fresh_ref, partial_ref):
+    n_chip, rows, width = part_ref.shape
+    micro, span, depth = fresh_ref.shape
+    half = span // 2
+    place = pl.ds(pl.multiple_of(lax.axis_index("core") * half, half), half)
     for j in range(n_chip):
-        columns = slice(j * width, (j + 1) * width)
-        partial = dot(mine_ref[...], own_ref[:, columns]) + dot(got_ref[...], other_ref[:, columns])
-        partial_ref[j] = partial.astype(jnp.bfloat16)
+        more = dot(got_ref[...], other_ref[:, j * width : (j + 1) * width])
+        partial_ref[j, :rows] = (part_ref[j] + more).astype(jnp.bfloat16)
+        for m in range(micro):
+            partial_ref[j, rows:, m * depth : (m + 1) * depth] = fresh_ref[m, place, :]
 
 
 def enter_kernel(step, incoming_ref, inputs_ref, layer_ref, copies_ref):
@@ -164,9 +188,10 @@
     section = lax.axis_index("section")
     index = step - section
     total = layer_ref[...].astype(jnp.float32)
-    summed = pieces_ref[0].astype(jnp.float32)
+    rows = layer_ref.shape[0]
+    summed = pieces_ref[0, :rows].astype(jnp.float32)
     for j in range(1, pieces_ref.shape[0]):
-        summed += pieces_ref[j].astype(jnp.float32)
+        summed += pieces_ref[j, :rows].astype(jnp.float32)
     updated = (total + summed).astype(jnp.bfloat16)
     send_ref[...] = updated
     new_ref[...] = done_ref[...]
@@ -176,20 +201,11 @@
         new_ref[jnp.clip(index, 0, chunks - 1)] = updated
 
 
-def share_kernel(fresh_ref, copies_ref):
-    micro, span, _ = fresh_ref.shape
-    half = span // 2
-    rows = pl.ds(pl.multiple_of(lax.axis_index("core") * half, half), half)
-    for m in range(micro):
-        block = fresh_ref[m, rows, :]
-        for j in range(copies_ref.shape[0]):
-            copies_ref[j, m * half : (m + 1) * half, :] = block
-
-
 def pick_kernel(holders_ref, blocks_ref, mine_ref, other_ref):
     heads, micro = holders_ref.shape
     count = heads * micro
-    half = mine_ref.shape[1]
+    _, half, depth = mine_ref.shape
+    below = blocks_ref.shape[1] - half
     holders = [holders_ref[e // micro, e % micro] for e in range(count)]
     core = lax.axis_index("core")
     first = 2 * lax.axis_index("chip")
@@ -201,7 +217,9 @@
 
             @pl.when(here)
             def _(slot=slot, e=e, ref=ref):
-                ref[slot] = blocks_ref[e // micro, (e % micro) * half : (e % micro + 1) * half, :]
+                ref[slot] = blocks_ref[
+                    e // micro, below:, (e % micro) * depth : (e % micro + 1) * depth
+                ]
 
             slot = jnp.minimum(slot + here.astype(jnp.int32), SLOTS - 1)
 
@@ -221,47 +239,49 @@
     return pl.ds(pl.multiple_of((2 * chip + core) * width, width), width)
 
 
-def give_kernel(width, query_ref, pair_ref, give_query_ref, give_pair_ref, sems):
+def give_kernel(width, query_ref, pair_ref, cache_ref, out_ref, first_ref, second_ref, sems):
     other = 1 - lax.axis_index("core")
+    columns = query_ref.shape[1]
+    micro, length, depth = cache_ref.shape
+    n_chip = query_ref.shape[0] // (2 * width)
     copies = []
-    for j in range(query_ref.shape[0] // (2 * width)):
-        rows, here = strip(j, other, width), pl.ds(j * width, width)
-        copies.append((query_ref.at[rows], give_query_ref.at[here]))
-        copies.append((pair_ref.at[rows], give_pair_ref.at[here]))
+    for j in range(n_chip):
+        theirs, here = strip(j, other, width), pl.ds(j * width, width)
+        copies.append((query_ref.at[theirs], first_ref.at[here, pl.ds(0, columns)]))
+        copies.append((pair_ref.at[theirs], first_ref.at[here, pl.ds(columns, HD)]))
+        copies.append((out_ref.at[:, theirs], second_ref.at[:, here]))
+    for m in range(micro):
+        place = first_ref.at[pl.ds(n_chip * width, length), pl.ds(m * depth, depth)]
+        copies.append((cache_ref.at[m], place))
     move(copies, sems)
 
 
-def keep_kernel(width, query_ref, out_ref, own_query_ref, own_out_ref, give_out_ref, sems):
+def keep_kernel(
+    width, query_ref, pair_ref, cache_ref, out_ref, got_ref,
+    own_query_ref, other_query_ref, both_ref, context_ref, own_out_ref, sems,
+):
     core = lax.axis_index("core")
-    copies = []
-    for j in range(query_ref.shape[0] // (2 * width)):
-        mine, here = strip(j, core, width), pl.ds(j * width, width)
-        copies.append((query_ref.at[mine], own_query_ref.at[here]))
-        copies.append((out_ref.at[:, mine], own_out_ref.at[:, here]))
-        copies.append((out_ref.at[:, strip(j, 1 - core, width)], give_out_ref.at[:, here]))
-    move(copies, sems)
-
-
-def join_kernel(
-    n_chip, pair_ref, got_pair_ref, cache_ref, got_cache_ref, got_query_ref,
-    both_ref, context_ref, other_query_ref, sems,
-):
-    width = pair_ref.shape[0] // (2 * n_chip)
-    core = lax.axis_index("core")
-    length = cache_ref.shape[1]
-    mine, theirs = pl.ds(pl.multiple_of(core * HD, HD), HD), pl.ds(pl.multiple_of((1 - core) * HD, HD), HD)
+    columns = query_ref.shape[1]
+    micro, length, depth = cache_ref.shape
+    n_chip = query_ref.shape[0] // (2 * width)
+    side = pl.ds(0, n_chip * width)
+    own = pl.ds(pl.multiple_of(core * HD, HD), HD)
+    other = pl.ds(pl.multiple_of((1 - core) * HD, HD), HD)
     early = pl.ds(pl.multiple_of(core * length, length), length)
     late = pl.ds(pl.multiple_of((1 - core) * length, length), length)
     copies = [
-        (got_pair_ref, both_ref.at[:, theirs]),
-        (cache_ref, context_ref.at[:, early]),
-        (got_cache_ref, context_ref.at[:, late]),
-        (got_query_ref, other_query_ref),
+        (got_ref.at[side, pl.ds(0, columns)], other_query_ref),
+        (got_ref.at[side, pl.ds(columns, HD)], both_ref.at[:, other]),
     ]
+    for m in range(micro):
+        got = got_ref.at[pl.ds(n_chip * width, length), pl.ds(m * depth, depth)]
+        copies.append((got, context_ref.at[m, late]))
+        copies.append((cache_ref.at[m], context_ref.at[m, early]))
     for j in range(n_chip):
-        copies.append(
-            (pair_ref.at[strip(j, core, width)], both_ref.at[pl.ds(j * width, width), mine])
-        )
+        mine, here = strip(j, core, width), pl.ds(j * width, width)
+        copies.append((query_ref.at[mine], own_query_ref.at[here]))
+        copies.append((pair_ref.at[mine], both_ref.at[here, own]))
+        copies.append((out_ref.at[:, mine], own_out_ref.at[:, here]))
     move(copies, sems)
 
 
@@ -323,52 +343,69 @@
     angle = shape((chunks, rows, HD), f32)
     state = shape((micro, span, 2 * HD), bf16)
     done_shape = shape((chunks, rows, width), bf16)
-    cosines, sines, fresh, done = call(
-        functools.partial(table_kernel, parts), (angle, angle, state, done_shape), 2**20, 1, 0, 4
-    )(ctx_len)
-
-    give_query, give_pair = shuffle(
-        functools.partial(give_kernel, width), (vmem(side, columns), vmem(side, HD)), 2, 2 * n_chip
-    )(wq, wkv)
-    got_query, got_pair, got_cache = swap(give_query), swap(give_pair), swap(cache[0])
-    layer_in, cosines, sines, fresh, done, _ = lax.optimization_barrier(
-        (hidden_in[0, :rows], cosines, sines, fresh, done, give_query)
-    )
-    features = exchange(jnp.broadcast_to(layer_in[None], (n_chip, rows, width)))
-    features, w_query, w_out = lax.optimization_barrier((features, w_query, w_out))
-    wq, wo = slow(w_query[0]), slow(w_out[0])
-    wq_own, wo_own, give_out = shuffle(
+    packed = shape((rows, columns + 3 * HD), f32)
+    block = shape((rows, columns), bf16)
+    spread = shape((n_chip, rows, width), bf16)
+    cosines, sines, fresh, done, layer_in, copies = call(
+        functools.partial(table_kernel, parts),
+        (angle, angle, state, done_shape, block, spread),
+        2**20,
+        1,
+        1,
+        4,
+    )(ctx_len, inputs)
+
+    first, second = shuffle(
+        functools.partial(give_kernel, width),
+        (vmem(side + cache.shape[2], columns + HD), vmem(columns, side)),
+        4,
+        3 * n_chip + micro,
+    )(wq, wkv, held, wo)
+    first, second, copies = lax.optimization_barrier((first, second, copies))
+    got_first, got_second = swap(first), swap(second)
+    features = exchange(copies)
+    features, w_query, w_key_value, w_out, cache = lax.optimization_barrier(
+        (features, w_query, w_key_value, w_out, cache)
+    )
+    wq, wkv, wo, held = (slow(x[0]) for x in (w_query, w_key_value, w_out, cache))
+    wq_own, wq_other, w_pair, context, wo_own = shuffle(
         functools.partial(keep_kernel, width),
-        (vmem(side, columns), vmem(columns, side), vmem(columns, side)),
-        2,
-        3 * n_chip,
-    )(wq, wo)
-    got_out = swap(give_out)
-    w_pair, context, wq_other = shuffle(
-        functools.partial(join_kernel, n_chip),
-        (vmem(side, 2 * HD), vmem(micro, 2 * cache.shape[2], 2 * HD), vmem(side, columns)),
+        (
+            vmem(side, columns),
+            vmem(side, columns),
+            vmem(side, 2 * HD),
+            vmem(micro, 2 * cache.shape[2], 2 * HD),
+            vmem(columns, side),
+        ),
         5,
-        4 + n_chip,
-    )(wkv, slow(got_pair), held, slow(got_cache), slow(got_query))
+        3 * n_chip + 2 + 2 * micro,
+    )(wq, wkv, held, wo, got_first)
     wo_other = None
     wq_own, wo_own, w_pair, context, wq_other = (
         fast(v) for v in (wq_own, wo_own, w_pair, context, wq_other)
     )
 
-    packed = shape((rows, columns + 3 * HD), f32)
-    block = shape((rows, columns), bf16)
+    query_flops = rows * depth * columns
     project = call(
-        project_kernel, (packed, packed), rows * depth * 2 * (columns + HD), 0, 5, 4
-    )
-    finish = call(
-        out_kernel, shape((n_chip, rows, width), bf16), 2 * rows * columns * depth, 0, 4, 4
+        project_kernel,
+        (shape((rows, side), bf16), packed),
+        query_flops + rows * depth * 2 * HD,
+        0,
+        4,
+        4,
+    )
+    query = call(query_kernel, shape((rows, columns), f32), query_flops, 0, 2, 4)
+    out = call(out_kernel, shape((n_chip, rows, width), f32), query_flops, 0, 2, 4)
+    finish = call(finish_kernel, spread, query_flops, 0, 3, 4)
+    last = call(
+        last_kernel, shape((n_chip, rows + span // 2, width), bf16), query_flops, 0, 4, 4
     )
     for step in range(steps):
         if step > 0:
             if step < chunks:
                 layer_in, copies = call(
                     functools.partial(enter_kernel, step),
-                    (block, shape((n_chip, rows, width), bf16)),
+                    (block, spread),
                     2**20,
                     0,
                     2,
@@ -377,26 +414,26 @@
             else:
                 copies = jnp.broadcast_to(layer_in[None], (n_chip, rows, width))
             features = exchange(copies)
-        keep, give = project(features, gain, wq_own, wq_other, w_pair)
+        scaled, give = project(features, gain, wq_other, w_pair)
+        got = swap(give)
+        keep = query(scaled, wq_own)
         attend = call(
             functools.partial(attend_kernel, depth, step),
             (block, state),
             4 * rows * columns * (context.shape[1] + span),
             1,
-            6,
+            7,
             12,
         )
-        attended, fresh = attend(ctx_len, keep, swap(give), cosines, sines, context, fresh)
+        attended, fresh = attend(ctx_len, keep, give, got, cosines, sines, context, fresh)
+        got = swap(attended)
+        part = out(attended, wo_own)
         if step == 0:
-            wo_other = fast(shuffle(load_kernel, vmem(columns, side), 1, 1)(slow(got_out)))
-        partial = finish(attended, swap(attended), wo_own, wo_other)
-        if step + 1 == steps:
-            partial, fresh = lax.optimization_barrier((partial, fresh))
-            copies = call(
-                share_kernel, shape((n_chip, micro * span // 2, 2 * HD), bf16), 2**20, 0, 1, 4
-            )(fresh)
-            blocks = exchange(copies)
-        pieces = exchange(partial)
+            wo_other = fast(shuffle(load_kernel, vmem(columns, side), 1, 1)(got_second))
+        if step + 1 < steps:
+            pieces = exchange(finish(part, got, wo_other))
+        else:
+            pieces = exchange(last(part, got, wo_other, fresh))
         settle = call(
             functools.partial(settle_kernel, step), (block, done_shape), 2**20, 0, 3, 4
         )
@@ -410,7 +447,7 @@
     outputs = done.reshape(micro, span, width)
 
     slots = shape((SLOTS, span // 2, 2 * HD), bf16)
-    mine, other = call(pick_kernel, (slots, slots), 2**20, 1, 1, 4)(placement[0], blocks)
+    mine, other = call(pick_kernel, (slots, slots), 2**20, 1, 1, 4)(placement[0], pieces)
     other = swap(other)
     store = jnp.where(
         lax.axis_index("core") == 0,

time: 489 us -> 451 us (0.922)
  the two profiles are of different devices: /device:TPU:70 before, /device:TPU:71 now
where the time goes in v3:
time: 451 us; the launch traced here: 442 us
  blocking collectives  237 us (53%)
  Pallas kernels  78.7 us (17%)
  waiting for transfers between devices  68.7 us (15%)
  starting transfers between devices  53.2 us (12%)
    all_to_all x21, blocking collectives, exchange(): lax.all_to_all(flat, 'chip', split_axis=0, concat_axis=0, tiled=True)  237 us
    ppermute x10, waiting for transfers between devices, shards(): layer_in = lax.ppermute(send, 'section', route)  48.7 us
    ppermute x25, starting transfers between devices, swap(): return lax.ppermute(x, 'core', [(0, 1), (1, 0)])  40.5 us
    pallas_call x11, Pallas kernels, shards(): attend(ctx_len, keep, give, got, cosines, sines, context, fresh)  23.7 us
    all_to_all x1, waiting for transfers between devices, exchange(): lax.all_to_all(flat, 'chip', split_axis=0, concat_axis=0, tiled=True)  16.2 us
    pallas_call x11, Pallas kernels, shards(): scaled, give = project(features, gain, wq_other, w_pair)  13.2 us
    pallas_call x11, Pallas kernels, shards(): part = out(attended, wo_own)  9.31 us
    ppermute x10, starting transfers between devices, shards(): layer_in = lax.ppermute(send, 'section', route)  9.16 us
  transfers between devices with their start and end apart: 36, of which 22 were waited for; matrix products, arithmetic and copies ran while one was open for 0% of the time, Pallas kernels for 6%

profile of v3, /device:TPU:71, one launch (start us, length us, event | category | flops | bytes accessed | tf_op | source)
XLA Modules:
  0.0 442.2 jit_solution(15774177988145953673)
XLA Ops:
  3.3 4.2 shard_map.95
  8.4 13.6 %all_to_all.132.x_ref = bf16[8,64,512]{2,1,0:T(8,128)(2,1)S(1)} all-to-all(bf16[8,64,512]{2,1,0:T(8,128)(2,1)S(1)} %get-tuple-element.99), channel_id=1, replica_groups=mesh['section'=8,'chip'=8,'core'=2] {'chip'}, dimensions={0} | all-to-all | bytes 1048576 | tf_op jit(solution)/shard_map/all_to_all | solution.py:24
  22.0 4.8 %shard_map.97 = (bf16[4096,512]{1,0:T(8,128)(2,1)S(1)}, bf16[4096,512]{1,0:T(8,128)(2,1)S(1)}, bf16[4096,256]{1,0:T(8,128)(2,1)S(1)}, bf16[2,2048,256]{2,1,0:T(8,128)(2,1)S(1)}, bf16[512,4096]{1,0:T(8,128)(2,1)S(1)}) custom-call(bf16[8192,512]{1,0:T(8,128)(2,1)} %bitcast.19, bf16[8192,128]{1,0:T(8,128)(2,1)} %bitcast.23, bf16[2,1024,256]{2,1,0:T(8,128)(2,1)} %bitcast.25, ...), custom_call_target="tpu_custom_call" | custom-call | tf_op jit(solution)/shard_map/pallas_call | solution.py:371
  36.0 11.8 %all_to_all.133.pieces_ref = bf16[8,64,512]{2,1,0:T(8,128)(2,1)S(1)} all-to-all(bf16[8,64,512]{2,1,0:T(8,128)(2,1)S(1)} %shard_map.103), channel_id=1, replica_groups=mesh['section'=8,'chip'=8,'core'=2] {'chip'}, dimensions={0} | all-to-all | bytes 1048576 | tf_op jit(solution)/shard_map/all_to_all | solution.py:24
  48.6 11.0 %all_to_all.134.x_ref = bf16[8,64,512]{2,1,0:T(8,128)(2,1)S(1)} all-to-all(bf16[8,64,512]{2,1,0:T(8,128)(2,1)S(1)} %get-tuple-element.121), channel_id=1, replica_groups=mesh['section'=8,'chip'=8,'core'=2] {'chip'}, dimensions={0} | all-to-all | bytes 1048576 | tf_op jit(solution)/shard_map/all_to_all | solution.py:24
  68.9 11.2 %all_to_all.135.pieces_ref = bf16[8,64,512]{2,1,0:T(8,128)(2,1)S(1)} all-to-all(bf16[8,64,512]{2,1,0:T(8,128)(2,1)S(1)} %shard_map.110), channel_id=1, replica_groups=mesh['section'=8,'chip'=8,'core'=2] {'chip'}, dimensions={0} | all-to-all | bytes 1048576 | tf_op jit(solution)/shard_map/all_to_all | solution.py:24
  80.9 11.9 %all_to_all.136.x_ref = bf16[8,64,512]{2,1,0:T(8,128)(2,1)S(1)} all-to-all(bf16[8,64,512]{2,1,0:T(8,128)(2,1)S(1)} %get-tuple-element.129), channel_id=1, replica_groups=mesh['section'=8,'chip'=8,'core'=2] {'chip'}, dimensions={0} | all-to-all | bytes 1048576 | tf_op jit(solution)/shard_map/all_to_all | solution.py:24
  102.3 11.2 %all_to_all.137.pieces_ref = bf16[8,64,512]{2,1,0:T(8,128)(2,1)S(1)} all-to-all(bf16[8,64,512]{2,1,0:T(8,128)(2,1)S(1)} %shard_map.117), channel_id=1, replica_groups=mesh['section'=8,'chip'=8,'core'=2] {'chip'}, dimensions={0} | all-to-all | bytes 1048576 | tf_op jit(solution)/shard_map/all_to_all | solution.py:24
  114.3 11.5 %all_to_all.138.x_ref = bf16[8,64,512]{2,1,0:T(8,128)(2,1)S(1)} all-to-all(bf16[8,64,512]{2,1,0:T(8,128)(2,1)S(1)} %get-tuple-element.137), channel_id=1, replica_groups=mesh['section'=8,'chip'=8,'core'=2] {'chip'}, dimensions={0} | all-to-all | bytes 1048576 | tf_op jit(solution)/shard_map/all_to_all | solution.py:24
  135.2 11.2 %all_to_all.139.pieces_ref = bf16[8,64,512]{2,1,0:T(8,128)(2,1)S(1)} all-to-all(bf16[8,64,512]{2,1,0:T(8,128)(2,1)S(1)} %shard_map.124), channel_id=1, replica_groups=mesh['section'=8,'chip'=8,'core'=2] {'chip'}, dimensions={0} | all-to-all | bytes 1048576 | tf_op jit(solution)/shard_map/all_to_all | solution.py:24
  147.2 11.5 %all_to_all.140.x_ref = bf16[8,64,512]{2,1,0:T(8,128)(2,1)S(1)} all-to-all(bf16[8,64,512]{2,1,0:T(8,128)(2,1)S(1)} %broadcast_in_dim.14), channel_id=1, replica_groups=mesh['section'=8,'chip'=8,'core'=2] {'chip'}, dimensions={0} | all-to-all | bytes 1048576 | tf_op jit(solution)/shard_map/all_to_all | solution.py:24
  168.3 11.2 %all_to_all.141.pieces_ref = bf16[8,64,512]{2,1,0:T(8,128)(2,1)S(1)} all-to-all(bf16[8,64,512]{2,1,0:T(8,128)(2,1)S(1)} %shard_map.130), channel_id=1, replica_groups=mesh['section'=8,'chip'=8,'core'=2] {'chip'}, dimensions={0} | all-to-all | bytes 1048576 | tf_op jit(solution)/shard_map/all_to_all | solution.py:24
  180.3 11.5 %all_to_all.142.x_ref = bf16[8,64,512]{2,1,0:T(8,128)(2,1)S(1)} all-to-all(bf16[8,64,512]{2,1,0:T(8,128)(2,1)S(1)} %broadcast_in_dim.15), channel_id=1, replica_groups=mesh['section'=8,'chip'=8,'core'=2] {'chip'}, dimensions={0} | all-to-all | bytes 1048576 | tf_op jit(solution)/shard_map/all_to_all | solution.py:24
  201.2 11.2 %all_to_all.143.pieces_ref = bf16[8,64,512]{2,1,0:T(8,128)(2,1)S(1)} all-to-all(bf16[8,64,512]{2,1,0:T(8,128)(2,1)S(1)} %shard_map.136), channel_id=1, replica_groups=mesh['section'=8,'chip'=8,'core'=2] {'chip'}, dimensions={0} | all-to-all | bytes 1048576 | tf_op jit(solution)/shard_map/all_to_all | solution.py:24
  213.3 11.5 %all_to_all.144.x_ref = bf16[8,64,512]{2,1,0:T(8,128)(2,1)S(1)} all-to-all(bf16[8,64,512]{2,1,0:T(8,128)(2,1)S(1)} %broadcast_in_dim.16), channel_id=1, replica_groups=mesh['section'=8,'chip'=8,'core'=2] {'chip'}, dimensions={0} | all-to-all | bytes 1048576 | tf_op jit(solution)/shard_map/all_to_all | solution.py:24
  234.1 11.3 %all_to_all.145.pieces_ref = bf16[8,64,512]{2,1,0:T(8,128)(2,1)S(1)} all-to-all(bf16[8,64,512]{2,1,0:T(8,128)(2,1)S(1)} %shard_map.142), channel_id=1, replica_groups=mesh['section'=8,'chip'=8,'core'=2] {'chip'}, dimensions={0} | all-to-all | bytes 1048576 | tf_op jit(solution)/shard_map/all_to_all | solution.py:24
  246.8 27.3 %collective-permute-done.22.layer_ref = bf16[64,512]{1,0:T(8,128)(2,1)S(1)} collective-permute-done((bf16[64,512]{1,0:T(8,128)(2,1)S(1)}, bf16[64,512]{1,0:T(8,128)(2,1)S(1)}, u32[]{:S(2)}, u32[]{:S(2)}) %collective-permute-start.22) | collective-permute-done | bytes 65568 | tf_op jit(solution)/shard_map/ppermute | solution.py:446
  274.1 10.1 %all_to_all.146.x_ref = bf16[8,64,512]{2,1,0:T(8,128)(2,1)S(1)} all-to-all(bf16[8,64,512]{2,1,0:T(8,128)(2,1)S(1)} %broadcast_in_dim.17), channel_id=1, replica_groups=mesh['section'=8,'chip'=8,'core'=2] {'chip'}, dimensions={0} | all-to-all | bytes 1048576 | tf_op jit(solution)/shard_map/all_to_all | solution.py:24
  285.4 3.7 collective-permute-start.23
  294.6 11.1 %all_to_all.147.pieces_ref = bf16[8,64,512]{2,1,0:T(8,128)(2,1)S(1)} all-to-all(bf16[8,64,512]{2,1,0:T(8,128)(2,1)S(1)} %shard_map.148), channel_id=1, replica_groups=mesh['section'=8,'chip'=8,'core'=2] {'chip'}, dimensions={0} | all-to-all | bytes 1048576 | tf_op jit(solution)/shard_map/all_to_all | solution.py:24
  307.1 8.4 %collective-permute-done.25.layer_ref = bf16[64,512]{1,0:T(8,128)(2,1)S(1)} collective-permute-done((bf16[64,512]{1,0:T(8,128)(2,1)S(1)}, bf16[64,512]{1,0:T(8,128)(2,1)S(1)}, u32[]{:S(2)}, u32[]{:S(2)}) %collective-permute-start.25) | collective-permute-done | bytes 65568 | tf_op jit(solution)/shard_map/ppermute | solution.py:446
  315.6 10.7 %all_to_all.148.x_ref = bf16[8,64,512]{2,1,0:T(8,128)(2,1)S(1)} all-to-all(bf16[8,64,512]{2,1,0:T(8,128)(2,1)S(1)} %broadcast_in_dim.18), channel_id=1, replica_groups=mesh['section'=8,'chip'=8,'core'=2] {'chip'}, dimensions={0} | all-to-all | bytes 1048576 | tf_op jit(solution)/shard_map/all_to_all | solution.py:24
  327.4 3.7 collective-permute-start.26
  336.6 11.1 %all_to_all.149.pieces_ref = bf16[8,64,512]{2,1,0:T(8,128)(2,1)S(1)} all-to-all(bf16[8,64,512]{2,1,0:T(8,128)(2,1)S(1)} %shard_map.154), channel_id=1, replica_groups=mesh['section'=8,'chip'=8,'core'=2] {'chip'}, dimensions={0} | all-to-all | bytes 1048576 | tf_op jit(solution)/shard_map/all_to_all | solution.py:24
  349.1 7.3 %collective-permute-done.28.layer_ref = bf16[64,512]{1,0:T(8,128)(2,1)S(1)} collective-permute-done((bf16[64,512]{1,0:T(8,128)(2,1)S(1)}, bf16[64,512]{1,0:T(8,128)(2,1)S(1)}, u32[]{:S(2)}, u32[]{:S(2)}) %collective-permute-start.28) | collective-permute-done | bytes 65568 | tf_op jit(solution)/shard_map/ppermute | solution.py:446
  356.5 10.7 %all_to_all.150.x_ref = bf16[8,64,512]{2,1,0:T(8,128)(2,1)S(1)} all-to-all(bf16[8,64,512]{2,1,0:T(8,128)(2,1)S(1)} %broadcast_in_dim.19), channel_id=1, replica_groups=mesh['section'=8,'chip'=8,'core'=2] {'chip'}, dimensions={0} | all-to-all | bytes 1048576 | tf_op jit(solution)/shard_map/all_to_all | solution.py:24
  368.4 3.7 collective-permute-start.29
  377.8 11.1 %all_to_all.151.pieces_ref = bf16[8,64,512]{2,1,0:T(8,128)(2,1)S(1)} all-to-all(bf16[8,64,512]{2,1,0:T(8,128)(2,1)S(1)} %shard_map.160), channel_id=1, replica_groups=mesh['section'=8,'chip'=8,'core'=2] {'chip'}, dimensions={0} | all-to-all | bytes 1048576 | tf_op jit(solution)/shard_map/all_to_all | solution.py:24
  390.3 5.7 %collective-permute-done.31.layer_ref = bf16[64,512]{1,0:T(8,128)(2,1)S(1)} collective-permute-done((bf16[64,512]{1,0:T(8,128)(2,1)S(1)}, bf16[64,512]{1,0:T(8,128)(2,1)S(1)}, u32[]{:S(2)}, u32[]{:S(2)}) %collective-permute-start.31) | collective-permute-done | bytes 65568 | tf_op jit(solution)/shard_map/ppermute | solution.py:446
  396.0 10.7 %all_to_all.152.x_ref = bf16[8,64,512]{2,1,0:T(8,128)(2,1)S(1)} all-to-all(bf16[8,64,512]{2,1,0:T(8,128)(2,1)S(1)} %broadcast_in_dim.20), channel_id=1, replica_groups=mesh['section'=8,'chip'=8,'core'=2] {'chip'}, dimensions={0} | all-to-all | bytes 1048576 | tf_op jit(solution)/shard_map/all_to_all | solution.py:24
  407.9 3.7 collective-permute-start.32
  421.8 16.2 %all-to-all-done.21.pieces_ref.blocks_ref = bf16[8,128,512]{2,1,0:T(8,128)(2,1)S(1)} async-done(((bf16[8,128,512]{2,1,0:T(8,128)(2,1)}), bf16[8,128,512]{2,1,0:T(8,128)(2,1)S(1)}, u32[]{:S(2)}, u32[]{:S(2)}) %all-to-all-start.21) | async-done | bytes 1048608 | tf_op jit(solution)/shard_map/all_to_all | solution.py:24
  (156 shorter events, 114.6 us)
Async XLA Ops:
  7.6 14.4 %collective-permute-start = (bf16[5120,640]{1,0:T(8,128)(2,1)S(1)}, bf16[5120,640]{1,0:T(8,128)(2,1)S(1)}, u32[]{:S(2)}, u32[]{:S(2)}) collective-permute-start(bf16[5120,640]{1,0:T(8,128)(2,1)S(1)} %get-tuple-element.105), channel_id=1, source_target_pairs={{0,1},{1,0},{2,3},{3,2},{4,5},{5,4},{6,7},{7,6},{8,9},{9,8},{10,11... | collective-permute-start | bytes 19660808 | tf_op jit(solution)/shard_map/ppermute | solution.py:19
  8.3 25.6 %collective-permute-start.3 = (bf16[512,4096]{1,0:T(8,128)(2,1)S(1)}, bf16[512,4096]{1,0:T(8,128)(2,1)S(1)}, u32[]{:S(2)}, u32[]{:S(2)}) collective-permute-start(bf16[512,4096]{1,0:T(8,128)(2,1)S(1)} %get-tuple-element.117), channel_id=1, source_target_pairs={{0,1},{1,0},{2,3},{3,2},{4,5},{5,4},{6,7},{7,6},{8,9},{9,8},{10,11... | collective-permute-start | bytes 12582920 | tf_op jit(solution)/shard_map/ppermute | solution.py:19
  28.1 3.3 collective-permute-start.1
  33.5 1.6 collective-permute-start.2
  47.8 0.7 collective-permute-start.4
  60.7 3.8 collective-permute-start.5
  66.7 1.4 collective-permute-start.6
  94.1 3.9 collective-permute-start.8
  100.1 1.4 collective-permute-start.9
  127.0 3.9 collective-permute-start.11
  133.0 1.4 collective-permute-start.12
  159.9 3.9 collective-permute-start.14
  166.0 1.4 collective-permute-start.15
  193.0 3.9 collective-permute-start.17
  199.0 1.4 collective-permute-start.18
  212.5 0.7 collective-permute-start.19
  225.9 3.9 collective-permute-start.20
  231.9 1.4 collective-permute-start.21
  245.5 28.6 %collective-permute-start.22 = (bf16[64,512]{1,0:T(8,128)(2,1)S(1)}, bf16[64,512]{1,0:T(8,128)(2,1)S(1)}, u32[]{:S(2)}, u32[]{:S(2)}) collective-permute-start(bf16[64,512]{1,0:T(8,128)(2,1)S(1)} %get-tuple-element.162), channel_id=1, source_target_pairs={{48,64},{64,80},{80,96},{96,112},{49,65},{65,81},{81,97},{97,113},... | collective-permute-start | bytes 196616 | tf_op jit(solution)/shard_map/ppermute | solution.py:446
  285.4 4.8 %collective-permute-start.23 = (f32[64,896]{1,0:T(8,128)S(1)}, f32[64,896]{1,0:T(8,128)S(1)}, u32[]{:S(2)}, u32[]{:S(2)}) collective-permute-start(f32[64,896]{1,0:T(8,128)S(1)} %get-tuple-element.164.give_ref), channel_id=1, source_target_pairs={{0,1},{1,0},{2,3},{3,2},{4,5},{5,4},{6,7},{7,6},{8,9},{9,8},{10,11... | collective-permute-start | bytes 688136 | tf_op jit(solution)/shard_map/ppermute | solution.py:19
  292.3 1.4 collective-permute-start.24
  305.8 9.7 %collective-permute-start.25 = (bf16[64,512]{1,0:T(8,128)(2,1)S(1)}, bf16[64,512]{1,0:T(8,128)(2,1)S(1)}, u32[]{:S(2)}, u32[]{:S(2)}) collective-permute-start(bf16[64,512]{1,0:T(8,128)(2,1)S(1)} %get-tuple-element.168), channel_id=1, source_target_pairs={{64,80},{80,96},{96,112},{65,81},{81,97},{97,113},{66,82},{82,98},... | collective-permute-start | bytes 196616 | tf_op jit(solution)/shard_map/ppermute | solution.py:446
  327.4 4.8 %collective-permute-start.26 = (f32[64,896]{1,0:T(8,128)S(1)}, f32[64,896]{1,0:T(8,128)S(1)}, u32[]{:S(2)}, u32[]{:S(2)}) collective-permute-start(f32[64,896]{1,0:T(8,128)S(1)} %get-tuple-element.170.give_ref), channel_id=1, source_target_pairs={{0,1},{1,0},{2,3},{3,2},{4,5},{5,4},{6,7},{7,6},{8,9},{9,8},{10,11... | collective-permute-start | bytes 688136 | tf_op jit(solution)/shard_map/ppermute | solution.py:19
  334.4 1.4 collective-permute-start.27
  347.8 8.6 %collective-permute-start.28 = (bf16[64,512]{1,0:T(8,128)(2,1)S(1)}, bf16[64,512]{1,0:T(8,128)(2,1)S(1)}, u32[]{:S(2)}, u32[]{:S(2)}) collective-permute-start(bf16[64,512]{1,0:T(8,128)(2,1)S(1)} %get-tuple-element.174), channel_id=1, source_target_pairs={{80,96},{96,112},{81,97},{97,113},{82,98},{98,114},{83,99},{99,115... | collective-permute-start | bytes 196616 | tf_op jit(solution)/shard_map/ppermute | solution.py:446
  368.4 4.8 %collective-permute-start.29 = (f32[64,896]{1,0:T(8,128)S(1)}, f32[64,896]{1,0:T(8,128)S(1)}, u32[]{:S(2)}, u32[]{:S(2)}) collective-permute-start(f32[64,896]{1,0:T(8,128)S(1)} %get-tuple-element.176.give_ref), channel_id=1, source_target_pairs={{0,1},{1,0},{2,3},{3,2},{4,5},{5,4},{6,7},{7,6},{8,9},{9,8},{10,11... | collective-permute-start | bytes 688136 | tf_op jit(solution)/shard_map/ppermute | solution.py:19
  375.6 1.4 collective-permute-start.30
  389.0 7.0 %collective-permute-start.31 = (bf16[64,512]{1,0:T(8,128)(2,1)S(1)}, bf16[64,512]{1,0:T(8,128)(2,1)S(1)}, u32[]{:S(2)}, u32[]{:S(2)}) collective-permute-start(bf16[64,512]{1,0:T(8,128)(2,1)S(1)} %get-tuple-element.180), channel_id=1, source_target_pairs={{96,112},{97,113},{98,114},{99,115},{100,116},{101,117},{102,118},... | collective-permute-start | bytes 196616 | tf_op jit(solution)/shard_map/ppermute | solution.py:446
  407.9 4.8 %collective-permute-start.32 = (f32[64,896]{1,0:T(8,128)S(1)}, f32[64,896]{1,0:T(8,128)S(1)}, u32[]{:S(2)}, u32[]{:S(2)}) collective-permute-start(f32[64,896]{1,0:T(8,128)S(1)} %get-tuple-element.182.give_ref), channel_id=1, source_target_pairs={{0,1},{1,0},{2,3},{3,2},{4,5},{5,4},{6,7},{7,6},{8,9},{9,8},{10,11... | collective-permute-start | bytes 688136 | tf_op jit(solution)/shard_map/ppermute | solution.py:19
  414.9 1.4 collective-permute-start.33
  418.1 19.9 %all-to-all-start.21 = ((bf16[8,128,512]{2,1,0:T(8,128)(2,1)}), bf16[8,128,512]{2,1,0:T(8,128)(2,1)S(1)}, u32[]{:S(2)}, u32[]{:S(2)}) async-start(bf16[8,128,512]{2,1,0:T(8,128)(2,1)} %shard_map.166), calls=%async_computation.21 | async-start | bytes 2097152 | tf_op jit(solution)/shard_map/all_to_all | solution.py:24
  438.9 2.2 collective-permute-start.34
  (10 other events, 32.5 us)
